TPU v7x, 512 devices: a whole 4x4x16 slice. The times are simulated.
512 devices in a mesh: tm: 8 (over y_hi, x), vox: 32 (over z, y_lo), feat: 2 (over core).
Axes of the slice: x: 4, y: 4 (y_hi: 2, y_lo: 2; y = y_hi * 2 + y_lo), z: 16, core: 2. Of those that a mesh axis runs over, the one named last changes fastest.
Arguments:
- design_matrix: bfloat16 [1024, 4096], P(None, ('tm', 'feat')), may hold values from -6 to 6
- measured_signals: bfloat16 [1024, 16384], P('tm', 'vox'), may hold values from -6 to 6
- predictor_group_label: int32 [4096], P('vox'), may hold values from 0 to 3
- shrinkage_weights: float32 [2, 4], replicated, may hold values from 0.1 to 10
- target_shrink_choice: int32 [256], P('vox'), may hold values from 0 to 1
Outputs:
- trailing: float32 [2, 4096, 4096], P(None, ('tm', 'feat'), 'vox')
- right_sides: float32 [4096, 16384], P(('tm', 'feat'), 'vox')
All inputs are finite; a program needn't handle non-finite values.
Results may differ from a plain program's by a relative error of at most 0.0003.
Values may be sent and summed in bfloat16 or wider, within the bound.
A program may use at most 64 MiB of HBM per device.

v0:
```python
import math

import jax
import jax.numpy as jnp
from jax import lax
from jax.sharding import PartitionSpec as P

P_SIZE = 4096
PREDICTOR_GROUPS = 4
SHRINK_OPTIONS = 2
GROUP = 64


def spread(block, axis, owner):
    block = jnp.where(lax.axis_index(axis) == owner, block, jnp.zeros_like(block))
    return lax.psum(block, axis)


def local(
    design_matrix, measured_signals, predictor_group_label, shrinkage_weights, target_shrink_choice
):
    row_index = lax.axis_index(("tm", "feat"))
    column_index = lax.axis_index("vox")
    total_time, row_block = design_matrix.shape
    column_width = P_SIZE // lax.axis_size("vox")
    voxel_count = measured_signals.shape[1]
    source_row = column_index * column_width // row_block
    own_columns = lax.dynamic_slice_in_dim(
        design_matrix, column_index * column_width - source_row * row_block, column_width, 1
    )
    shared_columns = spread(own_columns, ("tm", "feat"), source_row)
    gram_tile = (
        jnp.einsum("tr,tc->rc", design_matrix, shared_columns, preferred_element_type=jnp.float32)
        / total_time
    )
    global_rows = row_index * row_block + jnp.arange(row_block)
    global_columns = column_index * column_width + jnp.arange(column_width)
    group_membership_mask = (
        predictor_group_label[:, None] == jnp.arange(PREDICTOR_GROUPS)[None, :]
    ).astype(jnp.float32)
    predictor_shrinkage = jnp.dot(
        shrinkage_weights, group_membership_mask.T, precision=lax.Precision.HIGHEST
    )
    on_diagonal = (global_rows[:, None] == global_columns[None, :])[None, :, :]
    system_tiles = gram_tile[None, :, :] + jnp.where(
        on_diagonal, predictor_shrinkage[:, None, :], 0.0
    )
    right_sides = jnp.einsum(
        "tr,tv->rv",
        design_matrix,
        lax.all_gather(measured_signals, "tm", axis=0, tiled=True),
        preferred_element_type=jnp.float32,
    )
    right_sides = right_sides / math.sqrt(total_time)
    first_ridge = jnp.repeat(target_shrink_choice, GROUP) == 0
    identity_block = jnp.broadcast_to(
        jnp.eye(column_width, dtype=jnp.float32), (SHRINK_OPTIONS, column_width, column_width)
    )
    diagonal_owner = 0 // row_block
    local_offset = 0 - diagonal_owner * row_block
    diagonal = system_tiles[:, local_offset : local_offset + column_width, :]
    diagonal = spread(diagonal, ("tm", "feat"), diagonal_owner)
    diagonal = jnp.where(column_index == 0, diagonal, identity_block)
    factor = jnp.linalg.cholesky(diagonal)
    solved = lax.linalg.triangular_solve(
        factor, system_tiles, left_side=False, lower=True, transpose_a=True
    )
    solved = jnp.where((global_rows >= 0)[None, :, None], solved, 0.0)
    panel, factor = (spread(solved, "vox", 0), spread(factor, "vox", 0))
    panel_slice = lax.dynamic_slice_in_dim(
        panel, column_index * column_width - source_row * row_block, column_width, 1
    )
    partner_rows = spread(panel_slice, ("tm", "feat"), source_row)
    block_sides = jnp.broadcast_to(
        right_sides[local_offset : local_offset + column_width],
        (SHRINK_OPTIONS, column_width, voxel_count),
    )
    solutions = lax.linalg.triangular_solve(factor, block_sides, left_side=True, lower=True)
    solved_sides = jnp.where(first_ridge[None, :], solutions[0], solutions[1])
    solved_sides = spread(solved_sides, ("tm", "feat"), diagonal_owner)
    system_tiles = system_tiles - jnp.einsum(
        "brk,bck->brc", panel, partner_rows, precision=lax.Precision.HIGHEST
    )
    update_first = jnp.dot(panel[0], solved_sides, precision=lax.Precision.HIGHEST)
    update_second = jnp.dot(panel[1], solved_sides, precision=lax.Precision.HIGHEST)
    right_sides = right_sides - jnp.where(first_ridge[None, :], update_first, update_second)
    inside_block = (global_rows >= 0) & (global_rows < column_width)
    placed = (
        jnp.zeros((row_block, voxel_count), jnp.float32)
        .at[local_offset : local_offset + column_width]
        .set(solved_sides)
    )
    right_sides = jnp.where(inside_block[:, None], placed, right_sides)
    return (system_tiles, right_sides)


def solution(mesh):
    return jax.shard_map(
        local,
        mesh=mesh,
        in_specs=(P(None, ("tm", "feat")), P("tm", "vox"), P("vox"), P(), P("vox")),
        out_specs=(P(None, ("tm", "feat"), "vox"), P(("tm", "feat"), "vox")),
        check_vma=False,
    )
```

profile of v0, /device:TPU:1, one launch (start us, length us, event | category | flops | bytes accessed | tf_op | source)
XLA Modules:
  0.0 824.0 jit_solution(15762308978932388789)
XLA Ops:
  8.0 0.0 copy-start
  8.0 0.0 copy-start.2
  8.0 0.0 all-reduce.8.cloned.1.call-start
  8.1 1.8 dynamic-slice_select_fusion
  9.9 0.0 all-reduce.8.cloned.1.call-update
  9.9 0.0 all-reduce.10.cloned.1.call-start
  10.0 0.0 copy-start.5
  10.0 0.0 copy-done
  10.0 0.6 copy-done.5
  10.6 0.2 convolution_bitcast_fusion
  10.8 0.2 broadcast_compare_fusion
  11.0 159.6 %all-reduce.8.cloned.1.call-done = bf16[1024,128]{1,0:T(8,128)(2,1)} async-done(((bf16[1024,128]{1,0:T(8,128)(2,1)}), bf16[1024,128]{1,0:T(8,128)(2,1)}) %all-reduce.8.cloned.1.call-update) | async-done | bytes 262160 | tf_op jit(solution)/shard_map/psum | solution.py:16
  170.6 0.0 copy-done.2
  170.6 1.2 fusion.3
  171.8 0.1 copy.12
  172.0 0.7 slice_select_fusion
  172.6 0.0 all-reduce.10.cloned.1.call-update
  172.7 0.0 all-reduce.12.cloned.1.call-start
  172.7 154.6 %all-reduce.10.cloned.1.call-done = f32[2,128,128]{2,1,0:T(8,128)} async-done(((f32[2,128,128]{2,1,0:T(8,128)}), f32[2,128,128]{2,1,0:T(8,128)}) %all-reduce.10.cloned.1.call-update) | async-done | bytes 131088 | tf_op jit(solution)/shard_map/psum | solution.py:16
  327.4 0.9 broadcast_select_fusion
  328.3 0.0 copy-start.4
  328.3 0.1 copy.13
  328.4 0.8 copy-done.4
  329.2 23.5 %custom-call.10 = f32[2,128,128]{2,1,0:T(8,128)S(1)} custom-call(f32[2,128,128]{2,1,0:T(8,128)S(1)} %fusion.11), custom_call_target="Cholesky" | custom-call | tf_op jit(solution)/shard_map/jit(cholesky)/cholesky | solution.py:64
  352.7 0.1 compare_reduce_fusion
  352.9 0.8 fusion.16
  353.6 19.7 %custom-call.11 = f32[2,1,128,128]{2,3,1,0:T(8,128)S(1)} custom-call(f32[2,1,128,128]{3,2,1,0:T(8,128)S(1)} %get-tuple-element.19), custom_call_target="InvertDiagBlocksLowerTriangular" | custom-call | tf_op jit(solution)/shard_map/triangular_solve | solution.py:65
  373.3 1.1 fusion.2
  374.4 0.0 all-reduce.12.cloned.1.call-update
  374.4 0.0 copy-start.6
  374.4 0.0 all-gather.2.cloned.1.call-start
  374.5 0.5 all-gather.2.cloned.1.call-update
  375.0 0.2 all-reduce.14.cloned.1.call-start
  375.2 0.0 copy-done.6
  375.3 0.1 broadcast_in_dim.93
  375.3 0.1 eq.69
  375.4 242.2 %all-reduce.12.cloned.1.call-done = (f32[2,256,128]{2,1,0:T(8,128)}, f32[2,128,128]{2,1,0:T(8,128)}) async-done(((f32[2,256,128]{2,1,0:T(8,128)}, f32[2,128,128]{2,1,0:T(8,128)}), (f32[2,256,128]{2,1,0:T(8,128)}, f32[2,128,128]{2,1,0:T(8,128)})) %all-reduce.12.cloned.1.call-update) | async-done | bytes 393232 | tf_op jit(solution)/shard_map/psum | solution.py:16
  617.6 1.0 select_bitcast_fusion
  618.6 19.7 %custom-call.12 = f32[2,1,128,128]{2,3,1,0:T(8,128)S(1)} custom-call(f32[2,1,128,128]{3,2,1,0:T(8,128)S(1)} %select_bitcast_fusion), custom_call_target="InvertDiagBlocksLowerTriangular" | custom-call | tf_op jit(solution)/shard_map/triangular_solve | solution.py:78
  638.3 0.7 dynamic-slice_select_fusion.1
  639.0 1.7 convolution_multiply_fusion
  640.7 0.6 fusion.6
  641.3 0.7 fusion.5
  642.0 0.0 all-reduce.14.cloned.1.call-update
  642.1 170.8 %all-reduce.14.cloned.1.call-done = (f32[2,128,128]{2,1,0:T(8,128)}, f32[128,512]{1,0:T(8,128)}) async-done(((f32[2,128,128]{2,1,0:T(8,128)}, f32[128,512]{1,0:T(8,128)}), (f32[2,128,128]{2,1,0:T(8,128)}, f32[128,512]{1,0:T(8,128)})) %all-reduce.14.cloned.1.call-update) | async-done | bytes 393232 | tf_op jit(solution)/shard_map/psum | solution.py:16
  812.9 2.0 convolution_subtract_fusion
  814.9 0.6 fusion.8
  815.5 1.4 fusion.1
  (17 shorter events, 0.2 us)
Async XLA Ops:
  8.0 2.0 copy-start
  8.0 162.6 %copy-start.2 = (bf16[1024,256]{1,0:T(8,128)(2,1)S(1)}, bf16[1024,256]{1,0:T(8,128)(2,1)}, u32[]{:S(2)}) copy-start(bf16[1024,256]{1,0:T(8,128)(2,1)} %param.7) | copy-start | bytes 1572868
  8.0 162.6 %all-reduce.8.cloned.1.call-start = ((), (), s32[]{:S(2)}) async-start(), calls=%async_computation | async-start | bytes 524288 | tf_op jit(solution)/shard_map/psum | solution.py:16
  9.9 317.5 %all-reduce.10.cloned.1.call-start = ((), (), s32[]{:S(2)}) async-start(), calls=%async_computation.1 | async-start | bytes 262144 | tf_op jit(solution)/shard_map/psum | solution.py:16
  10.0 0.7 copy-start.5
  172.7 445.0 %all-reduce.12.cloned.1.call-start = ((), (), s32[]{:S(2)}) async-start(), calls=%async_computation.3 | async-start | bytes 786432 | tf_op jit(solution)/shard_map/psum | solution.py:16
  328.3 0.9 copy-start.4
  374.4 0.8 copy-start.6
  374.4 264.5 %all-gather.2.cloned.1.call-start = ((), (), s32[]{:S(2)}) async-start(), calls=%async_computation.2 | async-start | bytes 1179648 | tf_op jit(solution)/shard_map/all_gather | solution.py:51
  375.0 437.9 %all-reduce.14.cloned.1.call-start = ((), (), s32[]{:S(2)}) async-start(), calls=%async_computation.4 | async-start | bytes 786432 | tf_op jit(solution)/shard_map/psum | solution.py:16
  617.6 20.7 %copy-start.1 = (f32[2,256,128]{2,1,0:T(8,128)S(1)}, f32[2,256,128]{2,1,0:T(8,128)}, u32[]{:S(2)}) copy-start(f32[2,256,128]{2,1,0:T(8,128)} %get-tuple-element.14) | copy-start | bytes 786436
  812.9 2.0 copy-start.3
Sparse Core Ops, SparseCore 0:
  12.3 158.2 all-reduce.7
  174.3 153.0 all-reduce.9
  374.5 243.0 all-reduce.11
  642.2 170.6 all-reduce.13
Sparse Core Ops, SparseCore 1:
  378.6 61.8 all-gather.1
where the time goes:
time: 824 us
  waiting for transfers between devices  728 us (88%)
  other arithmetic  69.7 us (8%)
  between operations  15.5 us (2%)
  matrix products  8.85 us (1%)
    psum x4, waiting for transfers between devices, spread(): return lax.psum(block, axis)  727 us
    another operation x4, other arithmetic, local(): factor = jnp.linalg.cholesky(diagonal)  23.6 us
    another operation x2, other arithmetic, local(): lax.linalg.triangular_solve(factor, block_sides, left_side=True, lower=True)  20.6 us
    another operation x2, other arithmetic, local(): lax.linalg.triangular_solve(factor, system_tiles, left_side=False, lower=...  19.7 us
  transfers between devices with their start and end apart: 5, of which 4 were waited for; matrix products, arithmetic and copies ran while one was open for 3% of the time, Pallas kernels for 0%

commit v1 on v0

v1 whole, which is shorter than its diff:
```python
import math

import jax
import jax.numpy as jnp
from jax import lax
from jax.experimental import pallas as pl
from jax.experimental.pallas import tpu as pltpu
from jax.sharding import PartitionSpec as P

TIME = 1024
GROUPS = 4
CB = 128
GROUP = 64
CHIPS = 8
OFFSETS = [(dy, dx) for dy in range(2) for dx in range(4)][1:]
MESH = pl.DeviceIdType.MESH


def peer(t, dy, dx):
    y, x = t // 4, t % 4
    return ((y + dy) % 2) * 4 + (x + dx) % 4


def remote(src, dst, send, recv, **where):
    return pltpu.make_async_remote_copy(
        src_ref=src, dst_ref=dst, send_sem=send, recv_sem=recv, device_id=where, device_id_type=MESH
    )


class Spread:
    def __init__(self, buf, t, f, to, fo, sem):
        self.buf, self.t, self.f, self.to, self.fo = buf, t, f, to, fo
        self.scatter, self.scatter_r, self.own, self.own_r, self.ag, self.ag_r, self.sib, self.sib_r = sem
        self.owner = (t == to) & (f == fo)
        self.relay = (t != to) & (f == fo)
        self.side = (t != to) & (f != fo)
        self.owner_side = (t == to) & (f != fo)

    def chunk(self, t):
        return self.buf.at[pl.ds(pl.multiple_of(t * 128, 128), 128), :]

    def c_scatter(self, k):
        p = peer(self.t, *OFFSETS[k])
        c = self.chunk(p)
        return remote(c, c, self.scatter.at[k], self.scatter_r, tm=p)

    def c_scatter_in(self):
        c = self.chunk(self.t)
        return remote(c, c, self.scatter.at[0], self.scatter_r, tm=self.to)

    def c_own(self, k):
        p = peer(self.t, *OFFSETS[k])
        c = self.chunk(self.t)
        return remote(c, c, self.own.at[k], self.own_r, tm=p)

    def c_own_in(self):
        c = self.chunk(self.to)
        return remote(c, c, self.own.at[0], self.own_r, tm=self.to)

    def c_ag(self, k):
        p = peer(self.t, *OFFSETS[k])
        c = self.chunk(self.t)
        return p, remote(c, c, self.ag.at[k], self.ag_r.at[k], tm=p)

    def c_ag_in(self, k):
        dy, dx = OFFSETS[k]
        p = peer(self.t, dy, 4 - dx)
        c = self.chunk(p)
        return p, remote(c, c, self.ag.at[k], self.ag_r.at[k], tm=p)

    def c_sib(self, k, p):
        c = self.chunk(p)
        return remote(c, c, self.sib.at[k], self.sib_r.at[k], feat=1 - self.f)

    def c_whole(self):
        return remote(self.buf, self.buf, self.sib.at[0], self.sib_r.at[0], feat=1 - self.f)

    def start(self):
        @pl.when(self.owner)
        def _():
            for k in range(7):
                self.c_scatter(k).start()
            for k in range(7):
                self.c_own(k).start()
            self.c_whole().start()

    def forward(self):
        @pl.when(self.relay)
        def _():
            self.c_scatter_in().wait_recv()
            for k in range(7):
                p, c = self.c_ag(k)

                @pl.when(p != self.to)
                def _():
                    c.start()

            self.c_sib(7, self.t).start()

    def collect(self):
        @pl.when(self.relay)
        def _():
            for k in range(7):
                p, c = self.c_ag_in(k)

                @pl.when(p != self.to)
                def _():
                    c.wait_recv()

                @pl.when(p == self.to)
                def _():
                    self.c_own_in().wait_recv()

                self.c_sib(k, p).start()

    def finish(self):
        @pl.when(self.owner)
        def _():
            for k in range(7):
                self.c_scatter(k).wait_send()
                self.c_own(k).wait_send()
            self.c_whole().wait_send()

        @pl.when(self.owner_side)
        def _():
            self.c_whole().wait_recv()

        @pl.when(self.relay)
        def _():
            for k in range(7):
                p, c = self.c_ag(k)

                @pl.when(p != self.to)
                def _():
                    c.wait_send()

                q, _c = self.c_ag_in(k)
                self.c_sib(k, q).wait_send()
            self.c_sib(7, self.t).wait_send()

        @pl.when(self.side)
        def _():
            for k in range(7):
                dy, dx = OFFSETS[k]
                self.c_sib(k, peer(self.t, dy, 4 - dx)).wait_recv()
            self.c_sib(7, self.t).wait_recv()


def spread_sems():
    dma = pltpu.SemaphoreType.DMA
    return [dma((7,)), dma, dma((7,)), dma, dma((7,)), dma((7,)), dma((8,)), dma((8,))]


def gather_kernel(a_ref, y_ref, lab_ref, s_ref, c_ref, yall_ref, labs_ref, *sems):
    s_sem, c_sem, rest = sems[:8], sems[8:16], sems[16:]
    ysend, yrecv, bsend, brecv, l1s, l1r, l2s, l2r, l3s, l3r = rest
    t, f, v = lax.axis_index("tm"), lax.axis_index("feat"), lax.axis_index("vox")
    row = t * 2 + f
    first_row, first_vox = row == 0, v == 0

    barrier = pltpu.get_barrier_semaphore()
    for dy, dx in OFFSETS:
        pl.semaphore_signal(barrier, inc=1, device_id={"tm": peer(t, dy, dx)}, device_id_type=MESH)
    pl.semaphore_signal(barrier, inc=1, device_id={"feat": 1 - f}, device_id_type=MESH)

    @pl.when(first_row & (v != 0))
    def _():
        pl.semaphore_signal(
            barrier, inc=1, device_id={"tm": v // 4, "feat": (v // 2) % 2, "vox": 0}, device_id_type=MESH
        )

    @pl.when(first_row)
    def _():
        s_ref[...] = a_ref[:, 0:128]

    to, fo = v // 4, (v // 2) % 2

    @pl.when((t == to) & (f == fo))
    def _():
        c_ref[...] = a_ref[:, pl.ds(pl.multiple_of((v % 2) * 128, 128), 128)]

    yall_ref[pl.ds(pl.multiple_of(t * 128, 128), 128), :] = y_ref[...]

    @pl.when(first_row & first_vox)
    def _():
        labs_ref[...] = lab_ref[...]

    @pl.when(v != 0)
    def _():
        pl.semaphore_wait(barrier, 8)

    @pl.when(first_vox & (row != 0))
    def _():
        pl.semaphore_wait(barrier, 10)

    @pl.when(first_vox & (row == 0))
    def _():
        pl.semaphore_wait(barrier, 9)

    def c_l1(i):
        return remote(lab_ref, labs_ref, l1s.at[i], l1r, tm=0, feat=0, vox=row * 2 + i)

    @pl.when(first_vox)
    def _():
        @pl.when(row != 0)
        def _():
            c_l1(0).start()

        c_l1(1).start()

    spread_s = Spread(s_ref, t, f, 0, 0, s_sem)
    spread_c = Spread(c_ref, t, f, to, fo, c_sem)
    spread_s.start()
    spread_c.start()

    def yblock(q, g):
        return yall_ref.at[pl.ds(pl.multiple_of(q * 128 + g * 64, 64), 64), :]

    def c_y(k):
        b = yblock(t, f)
        return remote(b, b, ysend.at[k], yrecv.at[k], tm=peer(t, *OFFSETS[k]))

    def source(k):
        dy, dx = OFFSETS[k]
        return peer(t, dy, 4 - dx)

    def c_yin(k):
        b = yblock(source(k), f)
        return remote(b, b, ysend.at[k], yrecv.at[k], tm=source(k))

    def c_yout(k):
        b = yblock(source(k), f)
        return remote(b, b, bsend.at[k], brecv.at[k], feat=1 - f)

    def c_yside(k):
        b = yblock(source(k), 1 - f)
        return remote(b, b, bsend.at[k], brecv.at[k], feat=1 - f)

    for k in range(7):
        c_y(k).start()

    def c_l2(k):
        return remote(labs_ref, labs_ref, l2s.at[k], l2r, tm=peer(t, *OFFSETS[k]))

    def c_l2in():
        return remote(labs_ref, labs_ref, l2s.at[0], l2r, tm=0)

    def c_l3():
        return remote(labs_ref, labs_ref, l3s, l3r, feat=1 - f)

    spread_s.forward()
    spread_c.forward()

    @pl.when(first_row)
    def _():
        @pl.when(v != 0)
        def _():
            remote(lab_ref, labs_ref, l1s.at[0], l1r, tm=0, feat=0, vox=0).wait_recv()

        for k in range(7):
            c_l2(k).start()

    @pl.when((f == 0) & (t != 0))
    def _():
        c_l2in().wait_recv()

    @pl.when(f == 0)
    def _():
        c_l3().start()

    spread_s.collect()
    spread_c.collect()
    for k in range(7):
        c_yin(k).wait_recv()
        c_yout(k).start()
    spread_s.finish()
    spread_c.finish()

    @pl.when(f == 1)
    def _():
        c_l3().wait_recv()

    @pl.when(f == 0)
    def _():
        c_l3().wait_send()

    @pl.when(first_row)
    def _():
        for k in range(7):
            c_l2(k).wait_send()

    @pl.when(first_vox)
    def _():
        @pl.when(row != 0)
        def _():
            c_l1(0).wait_send()

        c_l1(1).wait_send()

    for k in range(7):
        c_y(k).wait_send()
        c_yout(k).wait_send()
        c_yside(k).wait_recv()


def gather(a, y, lab):
    dma = pltpu.SemaphoreType.DMA
    vmem = pl.BlockSpec(memory_space=pltpu.VMEM)
    voxels = y.shape[1]
    return pl.pallas_call(
        gather_kernel,
        out_shape=[
            jax.ShapeDtypeStruct((TIME, CB), jnp.bfloat16),
            jax.ShapeDtypeStruct((TIME, CB), jnp.bfloat16),
            jax.ShapeDtypeStruct((TIME, voxels), jnp.bfloat16),
            jax.ShapeDtypeStruct((1, CB), jnp.int32),
        ],
        in_specs=[vmem] * 3,
        out_specs=[vmem] * 4,
        scratch_shapes=spread_sems()
        + spread_sems()
        + [dma((7,)), dma((7,)), dma((7,)), dma((7,)), dma((2,)), dma, dma((7,)), dma, dma, dma],
        compiler_params=pltpu.CompilerParams(
            collective_id=0, has_side_effects=True, vmem_limit_bytes=16 << 20
        ),
        name="gather",
    )(a, y, lab)


def inverse_factor(matrix):
    n = matrix.shape[0]
    count = n // 8
    sub = lax.broadcasted_iota(jnp.int32, (8, n), 0)
    lane = lax.broadcasted_iota(jnp.int32, (8, n), 1)
    rows = [matrix[8 * i : 8 * i + 8, :] for i in range(count)]
    out = []
    for j in range(count):
        inside = (lane >= 8 * j) & (lane < 8 * j + 8)
        eye = jnp.where(lane == 8 * j + sub, 1.0, 0.0)
        cols = {}
        for i in range(j, count):
            r = rows[i]
            cols[i] = [jnp.broadcast_to(r[:, 8 * j + p : 8 * j + p + 1], (8, n)) for p in range(8)]
            rows[i] = jnp.where(inside, eye if i == j else 0.0, r)
        scale = jnp.zeros((8, n), jnp.float32)
        for p in range(8):
            crow = [jnp.broadcast_to(cols[j][k][p : p + 1, :], (8, n)) if k >= p else None for k in range(8)]
            rrow = jnp.broadcast_to(rows[j][p : p + 1, :], (8, n))
            inv = 1.0 / crow[p]
            scale = jnp.where(sub == p, lax.rsqrt(crow[p]), scale)
            for i in range(j, count):
                factor = cols[i][p] * inv
                if i == j:
                    factor = jnp.where(sub > p, factor, 0.0)
                rows[i] = rows[i] - factor * rrow
                for k in range(p + 1, 8):
                    cols[i][k] = cols[i][k] - factor * crow[k]
        out.append(jnp.where(lane <= 8 * j + sub, rows[j] * scale, 0.0))
    return out


def tdot(a, b):
    return lax.dot_general(a, b, (((0,), (0,)), ((), ())), preferred_element_type=jnp.float32)


def fdot(a, b):
    return jnp.dot(a, b, precision=lax.Precision.HIGHEST, preferred_element_type=jnp.float32)


def solve_kernel(
    weights_ref, choice_ref, a_ref, s_ref, c_ref, y_ref, labs_ref, labc_ref, trail_ref, sides_ref, inv_ref
):
    t, f, v = lax.axis_index("tm"), lax.axis_index("feat"), lax.axis_index("vox")
    row = t * 2 + f
    rows, voxels = sides_ref.shape
    s = s_ref[...]
    c = c_ref[...]
    y = y_ref[...]
    a = a_ref[...]

    def penalty(r, lab):
        total = jnp.zeros(lab.shape, jnp.float32)
        for g in range(GROUPS):
            total = jnp.where(lab == g, weights_ref[r, g], total)
        return total

    i_sub = lax.broadcasted_iota(jnp.int32, (CB, CB), 0)
    i_lane = lax.broadcasted_iota(jnp.int32, (CB, CB), 1)
    eye = i_sub == i_lane
    gss = tdot(s, s) * (1.0 / TIME)
    for r in range(2):
        pen = jnp.broadcast_to(penalty(r, labs_ref[...]), (CB, CB))
        for j, block in enumerate(inverse_factor(gss + jnp.where(eye, pen, 0.0))):
            inv_ref[r, 8 * j : 8 * j + 8, :] = block

    r_sub = lax.broadcasted_iota(jnp.int32, (rows, CB), 0) + row * rows
    r_lane = lax.broadcasted_iota(jnp.int32, (rows, CB), 1)
    grs = tdot(a, s) * (1.0 / TIME)
    grc = tdot(a, c) * (1.0 / TIME)
    gsc = tdot(s, c) * (1.0 / TIME)
    side = tdot(a, y) * (1.0 / math.sqrt(TIME))
    sside = tdot(s, y) * (1.0 / math.sqrt(TIME))

    group = lax.broadcasted_iota(jnp.int32, (1, voxels), 1) // GROUP
    ridge = jnp.zeros((1, voxels), jnp.int32)
    for g in range(voxels // GROUP):
        ridge = jnp.where(group == g, choice_ref[g], ridge)

    panels, solved = [], []
    for r in range(2):
        inv = inv_ref[r]
        pen_s = jnp.broadcast_to(penalty(r, labs_ref[...]), (rows, CB))
        pen_c = jnp.broadcast_to(penalty(r, labc_ref[...]), (rows, CB))
        grs_r = grs + jnp.where(r_sub == r_lane, pen_s, 0.0)
        gsc_r = gsc + jnp.where(eye & (v == 0), pen_c[:CB], 0.0)
        panel = lax.dot_general(
            grs_r, inv, (((1,), (1,)), ((), ())), precision=lax.Precision.HIGHEST,
            preferred_element_type=jnp.float32,
        )
        partner = fdot(inv, gsc_r)
        system = grc + jnp.where(r_sub == r_lane + v * CB, pen_c, 0.0)
        trail_ref[r] = system - fdot(panel, partner)
        panels.append(panel)
        solved.append(jnp.where(ridge == r, fdot(inv, sside), 0.0))
    update = fdot(panels[0], solved[0]) + fdot(panels[1], solved[1])
    sides_ref[...] = side - update

    @pl.when(row == 0)
    def _():
        sides_ref[0:CB, :] = solved[0] + solved[1]


def solve(weights, choice, a, s, c, y, labs, labc):
    vmem = pl.BlockSpec(memory_space=pltpu.VMEM)
    smem = pl.BlockSpec(memory_space=pltpu.SMEM)
    rows, voxels = a.shape[1], y.shape[1]
    return pl.pallas_call(
        solve_kernel,
        out_shape=[
            jax.ShapeDtypeStruct((2, rows, CB), jnp.float32),
            jax.ShapeDtypeStruct((rows, voxels), jnp.float32),
        ],
        in_specs=[smem, smem] + [vmem] * 6,
        out_specs=[vmem] * 2,
        scratch_shapes=[pltpu.VMEM((2, CB, CB), jnp.float32)],
        compiler_params=pltpu.CompilerParams(vmem_limit_bytes=32 << 20),
        name="solve",
    )(weights, choice, a, s, c, y, labs, labc)


def local(design, signals, label, weights, choice):
    lab = label.reshape(1, CB)
    s, c, y, labs = gather(design, signals, lab)
    trail, sides = solve(weights, choice, design, s, c, y, labs, lab)
    return trail, sides


def solution(mesh):
    return jax.shard_map(
        local,
        mesh=mesh,
        in_specs=(P(None, ("tm", "feat")), P("tm", "vox"), P("vox"), P(), P("vox")),
        out_specs=(P(None, ("tm", "feat"), "vox"), P(("tm", "feat"), "vox")),
        check_vma=False,
    )
```

time: 824 us -> 45.8 us (0.06)
  the two profiles are of different devices: /device:TPU:1 before, /device:TPU:5 now
where the time goes in v1:
time: 45.8 us; the launch traced here: 45.6 us
  Pallas kernels  41.6 us (91%)
  local copies, waits for them, and re-layouts  3.26 us (7%)
  between operations  0.67 us (1%)
    pallas_call x1, Pallas kernels, gather(): pl.pallas_call(gather_kernel, out_shape=[jax.ShapeDtypeStruct((TIME, CB),...  30 us
    pallas_call x1, Pallas kernels, solve(): pl.pallas_call(solve_kernel, out_shape=[jax.ShapeDtypeStruct((2, rows, CB...  11.6 us
    unnamed x12, local copies, waits for them, and re-layouts  3.26 us

profile of v1, /device:TPU:5, one launch (start us, length us, event | category | flops | bytes accessed | tf_op | source)
XLA Modules:
  0.0 45.6 jit_solution(11055818318654648004)
XLA Ops:
  0.6 0.0 copy-start.3
  0.6 0.6 %copy-done.3 = s32[128]{0:T(128)S(1)} copy-done((s32[128]{0:T(128)S(1)}, s32[128]{0:T(128)}, u32[]{:S(2)}) %copy-start.3) | copy-done | bytes 536
  1.3 0.0 copy-start
  1.3 1.0 %copy-done = bf16[1024,256]{1,0:T(8,128)(2,1)S(1)} copy-done((bf16[1024,256]{1,0:T(8,128)(2,1)S(1)}, bf16[1024,256]{1,0:T(8,128)(2,1)}, u32[]{:S(2)}) %copy-start) | copy-done | bytes 524312
  2.3 0.0 copy-start.2
  2.3 0.9 %copy-done.2 = bf16[128,512]{1,0:T(8,128)(2,1)S(1)} copy-done((bf16[128,512]{1,0:T(8,128)(2,1)S(1)}, bf16[128,512]{1,0:T(8,128)(2,1)}, u32[]{:S(2)}) %copy-start.2) | copy-done | bytes 131096
  3.2 0.0 copy-start.1
  3.2 30.0 %gather.1 = (bf16[1024,128]{1,0:T(8,128)(2,1)S(1)}, bf16[1024,128]{1,0:T(8,128)(2,1)S(1)}, bf16[1024,512]{1,0:T(8,128)(2,1)S(1)}, s32[1,128]{1,0:T(1,128)S(1)}) custom-call(bf16[1024,256]{1,0:T(8,128)(2,1)S(1)} %copy-done, bf16[128,512]{1,0:T(8,128)(2,1)S(1)} %copy-done.2, s32[1,128]{1,0:T(1,128)S(1)} %bitcast.1), custom_call_target="tpu_custom_call" | custom-call | tf_op jit(solution)/shard_map/gather/pallas_call | solution.py:310
  33.2 0.0 copy-start.4
  33.3 0.0 copy-start.5
  33.3 0.0 copy-done.1
  33.3 0.6 %copy-done.4 = f32[2,4]{1,0:T(2,128)S(1)} copy-done((f32[2,4]{1,0:T(2,128)S(1)}, f32[2,4]{1,0:T(2,128)}, u32[]{:S(2)}) %copy-start.4) | copy-done | bytes 56
  33.9 0.0 copy-done.5
  33.9 11.6 %solve.1 = (f32[2,256,128]{2,1,0:T(8,128)}, f32[256,512]{1,0:T(8,128)}) custom-call(f32[2,4]{1,0:T(2,128)S(1)} %copy-done.4, s32[8]{0:T(128)S(1)} %copy-done.5, bf16[1024,256]{1,0:T(8,128)(2,1)S(1)} %copy-done.1, bf16[1024,128]{1,0:T(8,128)(2,1)S(1)} %get-tuple-element.6.s_ref, bf16[1024,128]{1,0:T(8,128)(2,1)S(1)} %get-tuple-element.7.c_ref, ...), custom_call_target="tpu_custom_call" | custom-call | tf_op jit(solution)/shard_map/solve/pallas_call | solution.py:437
Async XLA Ops:
  0.6 0.7 %copy-start.3 = (s32[128]{0:T(128)S(1)}, s32[128]{0:T(128)}, u32[]{:S(2)}) copy-start(s32[128]{0:T(128)} %param.7) | copy-start | bytes 1540
  1.3 1.0 %copy-start = (bf16[1024,256]{1,0:T(8,128)(2,1)S(1)}, bf16[1024,256]{1,0:T(8,128)(2,1)}, u32[]{:S(2)}) copy-start(bf16[1024,256]{1,0:T(8,128)(2,1)} %a_ref.3) | copy-start | bytes 1572868
  2.3 0.9 %copy-start.2 = (bf16[128,512]{1,0:T(8,128)(2,1)S(1)}, bf16[128,512]{1,0:T(8,128)(2,1)}, u32[]{:S(2)}) copy-start(bf16[128,512]{1,0:T(8,128)(2,1)} %y_ref.1) | copy-start | bytes 393220
  3.2 30.0 %copy-start.1 = (bf16[1024,256]{1,0:T(8,128)(2,1)S(1)}, bf16[1024,256]{1,0:T(8,128)(2,1)}, u32[]{:S(2)}) copy-start(bf16[1024,256]{1,0:T(8,128)(2,1)} %a_ref.3) | copy-start | bytes 1572868
  33.2 0.7 %copy-start.4 = (f32[2,4]{1,0:T(2,128)S(1)}, f32[2,4]{1,0:T(2,128)}, u32[]{:S(2)}) copy-start(f32[2,4]{1,0:T(2,128)} %weights_ref.1) | copy-start | bytes 100
  33.3 0.7 %copy-start.5 = (s32[8]{0:T(128)S(1)}, s32[8]{0:T(128)}, u32[]{:S(2)}) copy-start(s32[8]{0:T(128)} %choice_ref.1) | copy-start | bytes 100

commit v2 on v1

--- a/solution.py
+++ b/solution.py
@@ -153,60 +153,90 @@
 
 def gather_kernel(a_ref, y_ref, lab_ref, s_ref, c_ref, yall_ref, labs_ref, *sems):
     s_sem, c_sem, rest = sems[:8], sems[8:16], sems[16:]
-    ysend, yrecv, bsend, brecv, l1s, l1r, l2s, l2r, l3s, l3r = rest
+    ysend, yrecv, bsend, brecv, lsend, lrecv, copy_sem = rest
     t, f, v = lax.axis_index("tm"), lax.axis_index("feat"), lax.axis_index("vox")
     row = t * 2 + f
-    first_row, first_vox = row == 0, v == 0
-
+    to, fo = v // 4, (v // 2) % 2
+    owner_s, owner_c = row == 0, (t == to) & (f == fo)
+    plain, server, single = v != 0, (v == 0) & (f == 1), (v == 0) & (f == 0)
     barrier = pltpu.get_barrier_semaphore()
-    for dy, dx in OFFSETS:
-        pl.semaphore_signal(barrier, inc=1, device_id={"tm": peer(t, dy, dx)}, device_id_type=MESH)
-    pl.semaphore_signal(barrier, inc=1, device_id={"feat": 1 - f}, device_id_type=MESH)
-
-    @pl.when(first_row & (v != 0))
-    def _():
-        pl.semaphore_signal(
-            barrier, inc=1, device_id={"tm": v // 4, "feat": (v // 2) % 2, "vox": 0}, device_id_type=MESH
-        )
-
-    @pl.when(first_row)
-    def _():
-        s_ref[...] = a_ref[:, 0:128]
-
-    to, fo = v // 4, (v // 2) % 2
-
-    @pl.when((t == to) & (f == fo))
-    def _():
-        c_ref[...] = a_ref[:, pl.ds(pl.multiple_of((v % 2) * 128, 128), 128)]
-
-    yall_ref[pl.ds(pl.multiple_of(t * 128, 128), 128), :] = y_ref[...]
-
-    @pl.when(first_row & first_vox)
-    def _():
-        labs_ref[...] = lab_ref[...]
-
-    @pl.when(v != 0)
+
+    def signal(**where):
+        pl.semaphore_signal(barrier, inc=1, device_id=where, device_id_type=MESH)
+
+    @pl.when(plain)
+    def _():
+        signal(tm=v // 4, feat=1, vox=0)
+
+    @pl.when(plain | single)
+    def _():
+        for dy, dx in OFFSETS:
+            signal(tm=peer(t, dy, dx))
+
+    @pl.when(plain | server)
+    def _():
+        signal(feat=1 - f)
+
+    get_s = pltpu.make_async_copy(a_ref.at[:, pl.ds(0, CB)], s_ref, copy_sem.at[0])
+    get_c = pltpu.make_async_copy(
+        a_ref.at[:, pl.ds(pl.multiple_of((v % 2) * CB, CB), CB)], c_ref, copy_sem.at[1]
+    )
+    get_y = pltpu.make_async_copy(
+        y_ref, yall_ref.at[pl.ds(pl.multiple_of(t * 128, 128), 128), :], copy_sem.at[2]
+    )
+    get_lab = pltpu.make_async_copy(lab_ref, labs_ref, copy_sem.at[3])
+
+    @pl.when(owner_s)
+    def _():
+        get_s.start()
+
+    @pl.when(owner_c)
+    def _():
+        get_c.start()
+
+    get_y.start()
+
+    @pl.when(v == 0)
+    def _():
+        get_lab.start()
+
+    @pl.when(owner_s)
+    def _():
+        get_s.wait()
+
+    @pl.when(owner_c)
+    def _():
+        get_c.wait()
+
+    get_y.wait()
+
+    @pl.when(v == 0)
+    def _():
+        get_lab.wait()
+
+    @pl.when(plain | single)
     def _():
         pl.semaphore_wait(barrier, 8)
 
-    @pl.when(first_vox & (row != 0))
-    def _():
-        pl.semaphore_wait(barrier, 10)
-
-    @pl.when(first_vox & (row == 0))
-    def _():
-        pl.semaphore_wait(barrier, 9)
-
-    def c_l1(i):
-        return remote(lab_ref, labs_ref, l1s.at[i], l1r, tm=0, feat=0, vox=row * 2 + i)
-
-    @pl.when(first_vox)
-    def _():
-        @pl.when(row != 0)
-        def _():
-            c_l1(0).start()
-
-        c_l1(1).start()
+    @pl.when(server & (t != 0))
+    def _():
+        pl.semaphore_wait(barrier, 64)
+
+    @pl.when(server & (t == 0))
+    def _():
+        pl.semaphore_wait(barrier, 48)
+
+    first = jnp.where(t == 0, 16, 0)
+
+    def c_lab(i):
+        where = dict(tm=i // 2 % 8, feat=i % 2, vox=t * 4 + i // 16)
+        return remote(labs_ref, labs_ref, lsend.at[i], lrecv, **where)
+
+    @pl.when(server)
+    def _():
+        @pl.loop(first, 64)
+        def _(i):
+            c_lab(i).start()
 
     spread_s = Spread(s_ref, t, f, 0, 0, s_sem)
     spread_c = Spread(c_ref, t, f, to, fo, c_sem)
@@ -216,96 +246,83 @@
     def yblock(q, g):
         return yall_ref.at[pl.ds(pl.multiple_of(q * 128 + g * 64, 64), 64), :]
 
-    def c_y(k):
-        b = yblock(t, f)
-        return remote(b, b, ysend.at[k], yrecv.at[k], tm=peer(t, *OFFSETS[k]))
+    def yslab(q):
+        return yall_ref.at[pl.ds(pl.multiple_of(q * 128, 128), 128), :]
 
     def source(k):
         dy, dx = OFFSETS[k]
         return peer(t, dy, 4 - dx)
 
-    def c_yin(k):
-        b = yblock(source(k), f)
-        return remote(b, b, ysend.at[k], yrecv.at[k], tm=source(k))
-
-    def c_yout(k):
-        b = yblock(source(k), f)
+    def c_y(k, b):
+        return remote(b, b, ysend.at[k], yrecv.at[k], tm=peer(t, *OFFSETS[k]))
+
+    def c_yout(k, b):
         return remote(b, b, bsend.at[k], brecv.at[k], feat=1 - f)
 
-    def c_yside(k):
-        b = yblock(source(k), 1 - f)
-        return remote(b, b, bsend.at[k], brecv.at[k], feat=1 - f)
-
-    for k in range(7):
-        c_y(k).start()
-
-    def c_l2(k):
-        return remote(labs_ref, labs_ref, l2s.at[k], l2r, tm=peer(t, *OFFSETS[k]))
-
-    def c_l2in():
-        return remote(labs_ref, labs_ref, l2s.at[0], l2r, tm=0)
-
-    def c_l3():
-        return remote(labs_ref, labs_ref, l3s, l3r, feat=1 - f)
+    @pl.when(plain)
+    def _():
+        for k in range(7):
+            c_y(k, yblock(t, f)).start()
+
+    @pl.when(single)
+    def _():
+        for k in range(7):
+            c_y(k, yslab(t)).start()
 
     spread_s.forward()
     spread_c.forward()
-
-    @pl.when(first_row)
-    def _():
-        @pl.when(v != 0)
-        def _():
-            remote(lab_ref, labs_ref, l1s.at[0], l1r, tm=0, feat=0, vox=0).wait_recv()
-
-        for k in range(7):
-            c_l2(k).start()
-
-    @pl.when((f == 0) & (t != 0))
-    def _():
-        c_l2in().wait_recv()
-
-    @pl.when(f == 0)
-    def _():
-        c_l3().start()
-
     spread_s.collect()
     spread_c.collect()
-    for k in range(7):
-        c_yin(k).wait_recv()
-        c_yout(k).start()
+
+    @pl.when(plain)
+    def _():
+        for k in range(7):
+            b = yblock(source(k), f)
+            c_y(k, b).wait_recv()
+            c_yout(k, b).start()
+
+    @pl.when(single)
+    def _():
+        for k in range(7):
+            b = yslab(source(k))
+            c_y(k, b).wait_recv()
+            c_yout(k, b).start()
+
     spread_s.finish()
     spread_c.finish()
 
-    @pl.when(f == 1)
-    def _():
-        c_l3().wait_recv()
-
-    @pl.when(f == 0)
-    def _():
-        c_l3().wait_send()
-
-    @pl.when(first_row)
-    def _():
-        for k in range(7):
-            c_l2(k).wait_send()
-
-    @pl.when(first_vox)
-    def _():
-        @pl.when(row != 0)
-        def _():
-            c_l1(0).wait_send()
-
-        c_l1(1).wait_send()
-
-    for k in range(7):
-        c_y(k).wait_send()
-        c_yout(k).wait_send()
-        c_yside(k).wait_recv()
+    @pl.when(plain)
+    def _():
+        for k in range(7):
+            c_y(k, yblock(t, f)).wait_send()
+            c_yout(k, yblock(source(k), f)).wait_send()
+            c_yout(k, yblock(source(k), 1 - f)).wait_recv()
+        c_lab(0).wait_recv()
+
+    @pl.when(single)
+    def _():
+        for k in range(7):
+            c_y(k, yslab(t)).wait_send()
+            c_yout(k, yslab(source(k))).wait_send()
+
+    @pl.when(server)
+    def _():
+        for k in range(7):
+            c_yout(k, yslab(source(k))).wait_recv()
+
+        @pl.loop(first, 64)
+        def _(i):
+            c_lab(i).wait_send()
+
+
+def in_hbm(*arrays):
+    return [pltpu.with_memory_space_constraint(x, pltpu.HBM) for x in arrays]
 
 
 def gather(a, y, lab):
     dma = pltpu.SemaphoreType.DMA
     vmem = pl.BlockSpec(memory_space=pltpu.VMEM)
+    hbm = pl.BlockSpec(memory_space=pltpu.HBM)
     voxels = y.shape[1]
     return pl.pallas_call(
         gather_kernel,
@@ -315,16 +332,16 @@
             jax.ShapeDtypeStruct((TIME, voxels), jnp.bfloat16),
             jax.ShapeDtypeStruct((1, CB), jnp.int32),
         ],
-        in_specs=[vmem] * 3,
+        in_specs=[hbm] * 3,
         out_specs=[vmem] * 4,
         scratch_shapes=spread_sems()
         + spread_sems()
-        + [dma((7,)), dma((7,)), dma((7,)), dma((7,)), dma((2,)), dma, dma((7,)), dma, dma, dma],
+        + [dma((7,)), dma((7,)), dma((7,)), dma((7,)), dma((64,)), dma, dma((4,))],
         compiler_params=pltpu.CompilerParams(
             collective_id=0, has_side_effects=True, vmem_limit_bytes=16 << 20
         ),
         name="gather",
-    )(a, y, lab)
+    )(*in_hbm(a, y, lab))
 
 
 def inverse_factor(matrix):
@@ -368,8 +385,16 @@
 
 
 def solve_kernel(
-    weights_ref, choice_ref, a_ref, s_ref, c_ref, y_ref, labs_ref, labc_ref, trail_ref, sides_ref, inv_ref
+    weights_hbm, choice_hbm, labc_hbm, a_ref, s_ref, c_ref, y_ref, labs_ref, trail_ref, sides_ref,
+    inv_ref, weights_ref, choice_ref, labc_ref, sem
 ):
+    small = [
+        pltpu.make_async_copy(weights_hbm, weights_ref, sem.at[0]),
+        pltpu.make_async_copy(choice_hbm, choice_ref, sem.at[1]),
+        pltpu.make_async_copy(labc_hbm, labc_ref, sem.at[2]),
+    ]
+    for copy in small:
+        copy.start()
     t, f, v = lax.axis_index("tm"), lax.axis_index("feat"), lax.axis_index("vox")
     row = t * 2 + f
     rows, voxels = sides_ref.shape
@@ -388,6 +413,8 @@
     i_lane = lax.broadcasted_iota(jnp.int32, (CB, CB), 1)
     eye = i_sub == i_lane
     gss = tdot(s, s) * (1.0 / TIME)
+    for copy in small:
+        copy.wait()
     for r in range(2):
         pen = jnp.broadcast_to(penalty(r, labs_ref[...]), (CB, CB))
         for j, block in enumerate(inverse_factor(gss + jnp.where(eye, pen, 0.0))):
@@ -430,9 +457,9 @@
         sides_ref[0:CB, :] = solved[0] + solved[1]
 
 
-def solve(weights, choice, a, s, c, y, labs, labc):
+def solve(weights, choice, labc, a, s, c, y, labs):
     vmem = pl.BlockSpec(memory_space=pltpu.VMEM)
-    smem = pl.BlockSpec(memory_space=pltpu.SMEM)
+    hbm = pl.BlockSpec(memory_space=pltpu.HBM)
     rows, voxels = a.shape[1], y.shape[1]
     return pl.pallas_call(
         solve_kernel,
@@ -440,18 +467,24 @@
             jax.ShapeDtypeStruct((2, rows, CB), jnp.float32),
             jax.ShapeDtypeStruct((rows, voxels), jnp.float32),
         ],
-        in_specs=[smem, smem] + [vmem] * 6,
+        in_specs=[hbm] * 3 + [vmem] * 5,
         out_specs=[vmem] * 2,
-        scratch_shapes=[pltpu.VMEM((2, CB, CB), jnp.float32)],
+        scratch_shapes=[
+            pltpu.VMEM((2, CB, CB), jnp.float32),
+            pltpu.SMEM(weights.shape, jnp.float32),
+            pltpu.SMEM(choice.shape, jnp.int32),
+            pltpu.VMEM((1, CB), jnp.int32),
+            pltpu.SemaphoreType.DMA((3,)),
+        ],
         compiler_params=pltpu.CompilerParams(vmem_limit_bytes=32 << 20),
         name="solve",
-    )(weights, choice, a, s, c, y, labs, labc)
+    )(*in_hbm(weights, choice, labc), a, s, c, y, labs)
 
 
 def local(design, signals, label, weights, choice):
     lab = label.reshape(1, CB)
     s, c, y, labs = gather(design, signals, lab)
-    trail, sides = solve(weights, choice, design, s, c, y, labs, lab)
+    trail, sides = solve(weights, choice, lab, design, s, c, y, labs)
     return trail, sides
 
 

time: 45.8 us -> 40.1 us (0.88)
  the two profiles are of different devices: /device:TPU:5 before, /device:TPU:3 now
where the time goes in v2:
time: 40.1 us; the launch traced here: 39.9 us
  Pallas kernels  39.3 us (98%)
  between operations  0.65 us (2%)
    pallas_call x1, Pallas kernels, gather(): pl.pallas_call(gather_kernel, out_shape=[jax.ShapeDtypeStruct((TIME, CB),...  27.7 us
    pallas_call x1, Pallas kernels, solve(): pl.pallas_call(solve_kernel, out_shape=[jax.ShapeDtypeStruct((2, rows, CB...  11.6 us

profile of v2, /device:TPU:3, one launch (start us, length us, event | category | flops | bytes accessed | tf_op | source)
XLA Modules:
  0.0 39.9 jit_solution(9643046099744538441)
XLA Ops:
  0.6 0.0 copy-start
  0.6 27.7 %gather.1 = (bf16[1024,128]{1,0:T(8,128)(2,1)S(1)}, bf16[1024,128]{1,0:T(8,128)(2,1)S(1)}, bf16[1024,512]{1,0:T(8,128)(2,1)S(1)}, s32[1,128]{1,0:T(1,128)S(1)}) custom-call(bf16[1024,256]{1,0:T(8,128)(2,1)} %a_ref.3, bf16[128,512]{1,0:T(8,128)(2,1)} %y_ref.1, s32[1,128]{1,0:T(1,128)} %bitcast.1), custom_call_target="tpu_custom_call" | custom-call | tf_op jit(solution)/shard_map/gather/pallas_call | solution.py:327
  28.3 0.0 copy-done
  28.3 11.6 %solve.1 = (f32[2,256,128]{2,1,0:T(8,128)}, f32[256,512]{1,0:T(8,128)}) custom-call(f32[2,4]{1,0:T(2,128)} %weights_hbm.1, s32[8]{0:T(128)} %choice_hbm.1, s32[1,128]{1,0:T(1,128)} %bitcast.2, bf16[1024,256]{1,0:T(8,128)(2,1)S(1)} %copy-done, bf16[1024,128]{1,0:T(8,128)(2,1)S(1)} %get-tuple-element.6.s_ref, bf16[1024,128]{1,0:T(8,128)(2,1)S(1)} %get-tuple-element.7.c_ref, ...), custom_call_target="tpu_custom_call" | custom-call | tf_op jit(solution)/shard_map/solve/pallas_call | solution.py:464
Async XLA Ops:
  0.6 27.7 %copy-start = (bf16[1024,256]{1,0:T(8,128)(2,1)S(1)}, bf16[1024,256]{1,0:T(8,128)(2,1)}, u32[]{:S(2)}) copy-start(bf16[1024,256]{1,0:T(8,128)(2,1)} %a_ref.3) | copy-start | bytes 1572868

commit v3 on v2

--- a/solution.py
+++ b/solution.py
@@ -113,6 +113,18 @@
 
                 self.c_sib(k, p).start()
 
+    def arrive(self):
+        @pl.when(self.owner_side)
+        def _():
+            self.c_whole().wait_recv()
+
+        @pl.when(self.side)
+        def _():
+            for k in range(7):
+                dy, dx = OFFSETS[k]
+                self.c_sib(k, peer(self.t, dy, 4 - dx)).wait_recv()
+            self.c_sib(7, self.t).wait_recv()
+
     def finish(self):
         @pl.when(self.owner)
         def _():
@@ -121,10 +133,6 @@
                 self.c_own(k).wait_send()
             self.c_whole().wait_send()
 
-        @pl.when(self.owner_side)
-        def _():
-            self.c_whole().wait_recv()
-
         @pl.when(self.relay)
         def _():
             for k in range(7):
@@ -138,20 +146,15 @@
                 self.c_sib(k, q).wait_send()
             self.c_sib(7, self.t).wait_send()
 
-        @pl.when(self.side)
-        def _():
-            for k in range(7):
-                dy, dx = OFFSETS[k]
-                self.c_sib(k, peer(self.t, dy, 4 - dx)).wait_recv()
-            self.c_sib(7, self.t).wait_recv()
-
 
 def spread_sems():
     dma = pltpu.SemaphoreType.DMA
     return [dma((7,)), dma, dma((7,)), dma, dma((7,)), dma((7,)), dma((8,)), dma((8,))]
 
 
-def gather_kernel(a_ref, y_ref, lab_ref, s_ref, c_ref, yall_ref, labs_ref, *sems):
+def gather_kernel(
+    a_ref, y_ref, lab_ref, w_hbm, s_ref, c_ref, yall_ref, labs_ref, inv_ref, w_ref, *sems
+):
     s_sem, c_sem, rest = sems[:8], sems[8:16], sems[16:]
     ysend, yrecv, bsend, brecv, lsend, lrecv, copy_sem = rest
     t, f, v = lax.axis_index("tm"), lax.axis_index("feat"), lax.axis_index("vox")
@@ -195,6 +198,8 @@
         get_c.start()
 
     get_y.start()
+    get_w = pltpu.make_async_copy(w_hbm, w_ref, copy_sem.at[4])
+    get_w.start()
 
     @pl.when(v == 0)
     def _():
@@ -209,6 +214,7 @@
         get_c.wait()
 
     get_y.wait()
+    get_w.wait()
 
     @pl.when(v == 0)
     def _():
@@ -259,35 +265,61 @@
     def c_yout(k, b):
         return remote(b, b, bsend.at[k], brecv.at[k], feat=1 - f)
 
-    @pl.when(plain)
-    def _():
-        for k in range(7):
-            c_y(k, yblock(t, f)).start()
-
-    @pl.when(single)
-    def _():
-        for k in range(7):
-            c_y(k, yslab(t)).start()
-
+    def y_start(ks):
+        @pl.when(plain)
+        def _():
+            for k in ks:
+                c_y(k, yblock(t, f)).start()
+
+        @pl.when(single)
+        def _():
+            for k in ks:
+                c_y(k, yslab(t)).start()
+
+    def y_collect(ks):
+        @pl.when(plain)
+        def _():
+            for k in ks:
+                b = yblock(source(k), f)
+                c_y(k, b).wait_recv()
+                c_yout(k, b).start()
+
+        @pl.when(single)
+        def _():
+            for k in ks:
+                b = yslab(source(k))
+                c_y(k, b).wait_recv()
+                c_yout(k, b).start()
+
+    y_start((0, 2))
     spread_s.forward()
     spread_c.forward()
+    y_start((3, 1, 4, 6, 5))
     spread_s.collect()
-    spread_c.collect()
+    spread_s.arrive()
 
     @pl.when(plain)
     def _():
-        for k in range(7):
-            b = yblock(source(k), f)
-            c_y(k, b).wait_recv()
-            c_yout(k, b).start()
-
-    @pl.when(single)
-    def _():
-        for k in range(7):
-            b = yslab(source(k))
-            c_y(k, b).wait_recv()
-            c_yout(k, b).start()
-
+        c_lab(0).wait_recv()
+
+    s_all = s_ref[...]
+    gram = tdot(s_all, s_all) * (1.0 / TIME)
+    eye = lax.broadcasted_iota(jnp.int32, (CB, CB), 0) == lax.broadcasted_iota(jnp.int32, (CB, CB), 1)
+    matrices = []
+    for r in range(2):
+        pen = jnp.broadcast_to(penalty(w_ref, r, labs_ref[...]), (CB, CB))
+        matrices.append(gram + jnp.where(eye, pen, 0.0))
+
+    def between(panel):
+        if panel == 0:
+            spread_c.collect()
+        elif panel == 1:
+            y_collect((0, 2, 3))
+        elif panel == 2:
+            y_collect((1, 4, 6, 5))
+
+    inverse_factor(jnp.stack(matrices), inv_ref, between)
+    spread_c.arrive()
     spread_s.finish()
     spread_c.finish()
 
@@ -297,7 +329,6 @@
             c_y(k, yblock(t, f)).wait_send()
             c_yout(k, yblock(source(k), f)).wait_send()
             c_yout(k, yblock(source(k), 1 - f)).wait_recv()
-        c_lab(0).wait_recv()
 
     @pl.when(single)
     def _():
@@ -319,7 +350,7 @@
     return [pltpu.with_memory_space_constraint(x, pltpu.HBM) for x in arrays]
 
 
-def gather(a, y, lab):
+def gather(a, y, lab, w):
     dma = pltpu.SemaphoreType.DMA
     vmem = pl.BlockSpec(memory_space=pltpu.VMEM)
     hbm = pl.BlockSpec(memory_space=pltpu.HBM)
@@ -331,49 +362,104 @@
             jax.ShapeDtypeStruct((TIME, CB), jnp.bfloat16),
             jax.ShapeDtypeStruct((TIME, voxels), jnp.bfloat16),
             jax.ShapeDtypeStruct((1, CB), jnp.int32),
+            jax.ShapeDtypeStruct((2, CB, CB), jnp.float32),
         ],
-        in_specs=[hbm] * 3,
-        out_specs=[vmem] * 4,
-        scratch_shapes=spread_sems()
+        in_specs=[hbm] * 4,
+        out_specs=[vmem] * 5,
+        scratch_shapes=[pltpu.SMEM(w.shape, jnp.float32)]
         + spread_sems()
-        + [dma((7,)), dma((7,)), dma((7,)), dma((7,)), dma((64,)), dma, dma((4,))],
+        + spread_sems()
+        + [dma((7,)), dma((7,)), dma((7,)), dma((7,)), dma((64,)), dma, dma((5,))],
         compiler_params=pltpu.CompilerParams(
-            collective_id=0, has_side_effects=True, vmem_limit_bytes=16 << 20
+            collective_id=0, has_side_effects=True, vmem_limit_bytes=24 << 20
         ),
         name="gather",
-    )(*in_hbm(a, y, lab))
-
-
-def inverse_factor(matrix):
-    n = matrix.shape[0]
-    count = n // 8
-    sub = lax.broadcasted_iota(jnp.int32, (8, n), 0)
-    lane = lax.broadcasted_iota(jnp.int32, (8, n), 1)
-    rows = [matrix[8 * i : 8 * i + 8, :] for i in range(count)]
+    )(*in_hbm(a, y, lab, w))
+
+
+PANEL = 32
+
+
+def eliminate(t, base):
+    q, height, n = t.shape
+    lane8 = lax.broadcasted_iota(jnp.int32, (q, 8, n), 2)
+    sub8 = lax.broadcasted_iota(jnp.int32, (q, 8, n), 1)
     out = []
-    for j in range(count):
-        inside = (lane >= 8 * j) & (lane < 8 * j + 8)
-        eye = jnp.where(lane == 8 * j + sub, 1.0, 0.0)
-        cols = {}
-        for i in range(j, count):
-            r = rows[i]
-            cols[i] = [jnp.broadcast_to(r[:, 8 * j + p : 8 * j + p + 1], (8, n)) for p in range(8)]
-            rows[i] = jnp.where(inside, eye if i == j else 0.0, r)
-        scale = jnp.zeros((8, n), jnp.float32)
+    for step in range(height // 8):
+        o = base + 8 * step
+        block = t[:, :8, :]
+        cols = [jnp.broadcast_to(block[:, :, o + p : o + p + 1], (q, 8, n)) for p in range(8)]
+        inside = (lane8 >= o) & (lane8 < o + 8)
+        block = jnp.where(inside, jnp.where(lane8 == o + sub8, 1.0, 0.0), block)
+        invs, rrows, crows = [], [], []
+        scale = jnp.zeros((q, 8, n), jnp.float32)
         for p in range(8):
-            crow = [jnp.broadcast_to(cols[j][k][p : p + 1, :], (8, n)) if k >= p else None for k in range(8)]
-            rrow = jnp.broadcast_to(rows[j][p : p + 1, :], (8, n))
+            crow = {k: jnp.broadcast_to(cols[k][:, p : p + 1, :], (q, 8, n)) for k in range(p, 8)}
+            rrow = jnp.broadcast_to(block[:, p : p + 1, :], (q, 8, n))
             inv = 1.0 / crow[p]
-            scale = jnp.where(sub == p, lax.rsqrt(crow[p]), scale)
-            for i in range(j, count):
-                factor = cols[i][p] * inv
-                if i == j:
-                    factor = jnp.where(sub > p, factor, 0.0)
-                rows[i] = rows[i] - factor * rrow
+            scale = jnp.where(sub8 == p, lax.rsqrt(crow[p]), scale)
+            factor = jnp.where(sub8 > p, cols[p] * inv, 0.0)
+            block = block - factor * rrow
+            for k in range(p + 1, 8):
+                cols[k] = cols[k] - factor * crow[k]
+            invs.append(inv)
+            rrows.append(rrow)
+            crows.append(crow)
+        out.append(block * scale)
+        rest = t.shape[1] - 8
+        if rest:
+            low = t[:, 8:, :].reshape(q, rest // 8, 8, n)
+            cols = [
+                jnp.broadcast_to(low[:, :, :, o + p : o + p + 1], (q, rest // 8, 8, n)) for p in range(8)
+            ]
+            lane = lax.broadcasted_iota(jnp.int32, low.shape, 3)
+            low = jnp.where((lane >= o) & (lane < o + 8), 0.0, low)
+            for p in range(8):
+                factor = cols[p] * invs[p][:, None]
+                low = low - factor * rrows[p][:, None]
                 for k in range(p + 1, 8):
-                    cols[i][k] = cols[i][k] - factor * crow[k]
-        out.append(jnp.where(lane <= 8 * j + sub, rows[j] * scale, 0.0))
-    return out
+                    cols[k] = cols[k] - factor * crows[p][k][:, None]
+            t = low.reshape(q, rest, n)
+    return jnp.concatenate(out, axis=1)
+
+
+def parts(x):
+    high = x.astype(jnp.bfloat16)
+    rest = x - high.astype(jnp.float32)
+    mid = rest.astype(jnp.bfloat16)
+    low = (rest - mid.astype(jnp.float32)).astype(jnp.bfloat16)
+    return high, mid, low
+
+
+def inverse_factor(t, out_ref, between):
+    q, n, _ = t.shape
+    lane = lax.broadcasted_iota(jnp.int32, (PANEL, n), 1)
+    sub = lax.broadcasted_iota(jnp.int32, (PANEL, n), 0)
+    for panel in range(n // PANEL):
+        base, end = panel * PANEL, (panel + 1) * PANEL
+        scaled = eliminate(t[:, :PANEL, :], base)
+        for r in range(q):
+            out_ref[r, base:end, :] = jnp.where(lane <= sub + base, scaled[r], 0.0)
+        if end < n:
+            rest = []
+            for r in range(q):
+                row = jnp.where((lane >= end) | (lane <= sub + base), scaled[r], 0.0)
+                h, m, l = parts(row)
+                update = tdot(
+                    jnp.concatenate([h, h, h, m, m, l], 0), jnp.concatenate([h, m, l, h, m, h], 0)
+                )[end:, :]
+                low = t[r, PANEL:, :]
+                lanes = lax.broadcasted_iota(jnp.int32, low.shape, 1)
+                rest.append(jnp.where((lanes >= base) & (lanes < end), 0.0, low) - update)
+            t = jnp.stack(rest)
+            between(panel)
+
+
+def penalty(w_ref, r, lab):
+    total = jnp.zeros(lab.shape, jnp.float32)
+    for g in range(GROUPS):
+        total = jnp.where(lab == g, w_ref[r, g], total)
+    return total
 
 
 def tdot(a, b):
@@ -385,8 +471,8 @@
 
 
 def solve_kernel(
-    weights_hbm, choice_hbm, labc_hbm, a_ref, s_ref, c_ref, y_ref, labs_ref, trail_ref, sides_ref,
-    inv_ref, weights_ref, choice_ref, labc_ref, sem
+    weights_hbm, choice_hbm, labc_hbm, a_ref, s_ref, c_ref, y_ref, labs_ref, inv_ref, trail_ref, sides_ref,
+    weights_ref, choice_ref, labc_ref, sem
 ):
     small = [
         pltpu.make_async_copy(weights_hbm, weights_ref, sem.at[0]),
@@ -403,23 +489,11 @@
     y = y_ref[...]
     a = a_ref[...]
 
-    def penalty(r, lab):
-        total = jnp.zeros(lab.shape, jnp.float32)
-        for g in range(GROUPS):
-            total = jnp.where(lab == g, weights_ref[r, g], total)
-        return total
-
     i_sub = lax.broadcasted_iota(jnp.int32, (CB, CB), 0)
     i_lane = lax.broadcasted_iota(jnp.int32, (CB, CB), 1)
     eye = i_sub == i_lane
-    gss = tdot(s, s) * (1.0 / TIME)
     for copy in small:
         copy.wait()
-    for r in range(2):
-        pen = jnp.broadcast_to(penalty(r, labs_ref[...]), (CB, CB))
-        for j, block in enumerate(inverse_factor(gss + jnp.where(eye, pen, 0.0))):
-            inv_ref[r, 8 * j : 8 * j + 8, :] = block
-
     r_sub = lax.broadcasted_iota(jnp.int32, (rows, CB), 0) + row * rows
     r_lane = lax.broadcasted_iota(jnp.int32, (rows, CB), 1)
     grs = tdot(a, s) * (1.0 / TIME)
@@ -436,8 +510,8 @@
     panels, solved = [], []
     for r in range(2):
         inv = inv_ref[r]
-        pen_s = jnp.broadcast_to(penalty(r, labs_ref[...]), (rows, CB))
-        pen_c = jnp.broadcast_to(penalty(r, labc_ref[...]), (rows, CB))
+        pen_s = jnp.broadcast_to(penalty(weights_ref, r, labs_ref[...]), (rows, CB))
+        pen_c = jnp.broadcast_to(penalty(weights_ref, r, labc_ref[...]), (rows, CB))
         grs_r = grs + jnp.where(r_sub == r_lane, pen_s, 0.0)
         gsc_r = gsc + jnp.where(eye & (v == 0), pen_c[:CB], 0.0)
         panel = lax.dot_general(
@@ -457,7 +531,7 @@
         sides_ref[0:CB, :] = solved[0] + solved[1]
 
 
-def solve(weights, choice, labc, a, s, c, y, labs):
+def solve(weights, choice, labc, a, s, c, y, labs, inv):
     vmem = pl.BlockSpec(memory_space=pltpu.VMEM)
     hbm = pl.BlockSpec(memory_space=pltpu.HBM)
     rows, voxels = a.shape[1], y.shape[1]
@@ -467,10 +541,9 @@
             jax.ShapeDtypeStruct((2, rows, CB), jnp.float32),
             jax.ShapeDtypeStruct((rows, voxels), jnp.float32),
         ],
-        in_specs=[hbm] * 3 + [vmem] * 5,
+        in_specs=[hbm] * 3 + [vmem] * 6,
         out_specs=[vmem] * 2,
         scratch_shapes=[
-            pltpu.VMEM((2, CB, CB), jnp.float32),
             pltpu.SMEM(weights.shape, jnp.float32),
             pltpu.SMEM(choice.shape, jnp.int32),
             pltpu.VMEM((1, CB), jnp.int32),
@@ -478,13 +551,13 @@
         ],
         compiler_params=pltpu.CompilerParams(vmem_limit_bytes=32 << 20),
         name="solve",
-    )(*in_hbm(weights, choice, labc), a, s, c, y, labs)
+    )(*in_hbm(weights, choice, labc), a, s, c, y, labs, inv)
 
 
 def local(design, signals, label, weights, choice):
     lab = label.reshape(1, CB)
-    s, c, y, labs = gather(design, signals, lab)
-    trail, sides = solve(weights, choice, lab, design, s, c, y, labs)
+    s, c, y, labs, inv = gather(design, signals, lab, weights)
+    trail, sides = solve(weights, choice, lab, design, s, c, y, labs, inv)
     return trail, sides
 
 

time: 40.1 us -> 36.1 us (0.900)
  the two profiles are of different devices: /device:TPU:3 before, /device:TPU:1 now
where the time goes in v3:
time: 36.1 us; the launch traced here: 35.9 us
  Pallas kernels  35.3 us (98%)
  between operations  0.65 us (2%)
    pallas_call x1, Pallas kernels, gather(): pl.pallas_call(gather_kernel, out_shape=[jax.ShapeDtypeStruct((TIME, CB),...  30.5 us
    pallas_call x1, Pallas kernels, solve(): pl.pallas_call(solve_kernel, out_shape=[jax.ShapeDtypeStruct((2, rows, CB...  4.82 us

profile of v3, /device:TPU:1, one launch (start us, length us, event | category | flops | bytes accessed | tf_op | source)
XLA Modules:
  0.0 35.9 jit_solution(6542912654186743719)
XLA Ops:
  0.6 0.0 copy-start
  0.6 30.5 %gather.1 = (bf16[1024,128]{1,0:T(8,128)(2,1)S(1)}, bf16[1024,128]{1,0:T(8,128)(2,1)S(1)}, bf16[1024,512]{1,0:T(8,128)(2,1)S(1)}, s32[1,128]{1,0:T(1,128)S(1)}, f32[2,128,128]{2,1,0:T(8,128)S(1)}) custom-call(bf16[1024,256]{1,0:T(8,128)(2,1)} %a_ref.3, bf16[128,512]{1,0:T(8,128)(2,1)} %y_ref.1, s32[1,128]{1,0:T(1,128)} %bitcast.1, f32[2,4]{1,0:T(2,128)} %weights_hbm.1), custom_call_target="tpu_custom_call" | custom-call | tf_op jit(solution)/shard_map/gather/pallas_call | solution.py:358
  31.1 0.0 copy-done
  31.1 4.8 %solve.1 = (f32[2,256,128]{2,1,0:T(8,128)}, f32[256,512]{1,0:T(8,128)}) custom-call(f32[2,4]{1,0:T(2,128)} %weights_hbm.1, s32[8]{0:T(128)} %choice_hbm.1, s32[1,128]{1,0:T(1,128)} %bitcast.2, bf16[1024,256]{1,0:T(8,128)(2,1)S(1)} %copy-done, bf16[1024,128]{1,0:T(8,128)(2,1)S(1)} %get-tuple-element.7.s_ref, bf16[1024,128]{1,0:T(8,128)(2,1)S(1)} %get-tuple-element.8.c_ref, ...), custom_call_target="tpu_custom_call" | custom-call | tf_op jit(solution)/shard_map/solve/pallas_call | solution.py:538
Async XLA Ops:
  0.6 30.5 %copy-start = (bf16[1024,256]{1,0:T(8,128)(2,1)S(1)}, bf16[1024,256]{1,0:T(8,128)(2,1)}, u32[]{:S(2)}) copy-start(bf16[1024,256]{1,0:T(8,128)(2,1)} %a_ref.3) | copy-start | bytes 1572868

commit v4 on v3

--- a/solution.py
+++ b/solution.py
@@ -11,9 +11,10 @@
 GROUPS = 4
 CB = 128
 GROUP = 64
-CHIPS = 8
-OFFSETS = [(dy, dx) for dy in range(2) for dx in range(4)][1:]
 MESH = pl.DeviceIdType.MESH
+NEAR = [(0, 1), (0, 3), (1, 0)]
+CHUNKS = 4
+CHUNK = TIME // CHUNKS
 
 
 def peer(t, dy, dx):
@@ -27,141 +28,193 @@
     )
 
 
-class Spread:
-    def __init__(self, buf, t, f, to, fo, sem):
-        self.buf, self.t, self.f, self.to, self.fo = buf, t, f, to, fo
-        self.scatter, self.scatter_r, self.own, self.own_r, self.ag, self.ag_r, self.sib, self.sib_r = sem
-        self.owner = (t == to) & (f == fo)
-        self.relay = (t != to) & (f == fo)
-        self.side = (t != to) & (f != fo)
-        self.owner_side = (t == to) & (f != fo)
-
-    def chunk(self, t):
-        return self.buf.at[pl.ds(pl.multiple_of(t * 128, 128), 128), :]
-
-    def c_scatter(self, k):
-        p = peer(self.t, *OFFSETS[k])
-        c = self.chunk(p)
-        return remote(c, c, self.scatter.at[k], self.scatter_r, tm=p)
-
-    def c_scatter_in(self):
-        c = self.chunk(self.t)
-        return remote(c, c, self.scatter.at[0], self.scatter_r, tm=self.to)
-
-    def c_own(self, k):
-        p = peer(self.t, *OFFSETS[k])
-        c = self.chunk(self.t)
-        return remote(c, c, self.own.at[k], self.own_r, tm=p)
-
-    def c_own_in(self):
-        c = self.chunk(self.to)
-        return remote(c, c, self.own.at[0], self.own_r, tm=self.to)
-
-    def c_ag(self, k):
-        p = peer(self.t, *OFFSETS[k])
-        c = self.chunk(self.t)
-        return p, remote(c, c, self.ag.at[k], self.ag_r.at[k], tm=p)
-
-    def c_ag_in(self, k):
-        dy, dx = OFFSETS[k]
-        p = peer(self.t, dy, 4 - dx)
-        c = self.chunk(p)
-        return p, remote(c, c, self.ag.at[k], self.ag_r.at[k], tm=p)
-
-    def c_sib(self, k, p):
-        c = self.chunk(p)
-        return remote(c, c, self.sib.at[k], self.sib_r.at[k], feat=1 - self.f)
-
-    def c_whole(self):
-        return remote(self.buf, self.buf, self.sib.at[0], self.sib_r.at[0], feat=1 - self.f)
-
-    def start(self):
+class Place:
+    def __init__(self):
+        self.t, self.f, self.v = lax.axis_index("tm"), lax.axis_index("feat"), lax.axis_index("vox")
+        self.zero = self.v == 0
+        self.mover = self.f == jnp.where(self.t == 0, 1, 0)
+        self.plain = self.v != 0
+        self.single = self.zero & self.mover
+        self.server = self.zero & jnp.logical_not(self.mover)
+
+    def core(self, t, own):
+        return jnp.where(self.zero, jnp.where(t == 0, 1, 0), own)
+
+    def near(self, k):
+        p = peer(self.t, *NEAR[k])
+        return dict(tm=p, feat=self.core(p, self.f))
+
+
+class Tree:
+    def __init__(self, here, buf, to, fo, plane, sem, extra=None):
+        self.here, self.buf, self.extra = here, buf, extra
+        self.send, self.recv, self.sib_send, self.sib_recv = sem
+        t = here.t
+        self.dx = (t % 4 - to % 4 + 4) % 4
+        self.dy = (t // 4 - to // 4 + 2) % 2
+        self.on = here.f == here.core(t, plane)
+        self.off = jnp.logical_not(self.on)
+        self.root = (self.dx == 0) & (self.dy == 0)
+        self.aside = self.root & here.plain & (fo != plane)
+        self.owner = self.on & self.root & here.plain & (fo == plane)
+        self.waits = jnp.logical_not(self.owner)
+
+    def chunk(self, i):
+        return self.buf.at[pl.ds(i * CHUNK, CHUNK), :]
+
+    def near(self, k, i):
+        c = self.chunk(i)
+        return remote(c, c, self.send.at[k * CHUNKS + i], self.recv.at[i], **self.here.near(k))
+
+    def sib(self, i):
+        c = self.chunk(i)
+        return remote(c, c, self.sib_send.at[i], self.sib_recv.at[i], feat=1 - self.here.f)
+
+    def sends(self, i, act):
+        out_right = (self.dx == 0) | (self.dx == 1) if i < CHUNKS // 2 else self.dx == 0
+        out_left = self.dx == 0 if i < CHUNKS // 2 else (self.dx == 0) | (self.dx == 3)
+
+        @pl.when(out_right)
+        def _():
+            act(self.near(0, i))
+
+        @pl.when(out_left)
+        def _():
+            act(self.near(1, i))
+
+        @pl.when(self.root & self.here.plain)
+        def _():
+            act(self.near(2, i))
+
+        @pl.when(jnp.logical_not(self.aside))
+        def _():
+            act(self.sib(i))
+
+    def across(self, i):
+        c = self.chunk(i)
+        return remote(c, c, self.sib_send.at[i], self.recv.at[i], feat=1 - self.here.f)
+
+    def ext(self, i, act):
+        c = self.chunk(i)
+        if self.extra is not None:
+
+            @pl.when(self.here.v == 1)
+            def _():
+                for n, (tm, feat) in enumerate(((0, 1), (4, 0))):
+                    act(remote(c, c, self.extra.at[n * CHUNKS + i], self.recv.at[i], tm=tm, feat=feat, vox=0))
+
+    def kick(self):
         @pl.when(self.owner)
         def _():
-            for k in range(7):
-                self.c_scatter(k).start()
-            for k in range(7):
-                self.c_own(k).start()
-            self.c_whole().start()
-
-    def forward(self):
-        @pl.when(self.relay)
-        def _():
-            self.c_scatter_in().wait_recv()
-            for k in range(7):
-                p, c = self.c_ag(k)
-
-                @pl.when(p != self.to)
-                def _():
-                    c.start()
-
-            self.c_sib(7, self.t).start()
-
-    def collect(self):
-        @pl.when(self.relay)
-        def _():
-            for k in range(7):
-                p, c = self.c_ag_in(k)
-
-                @pl.when(p != self.to)
-                def _():
-                    c.wait_recv()
-
-                @pl.when(p == self.to)
-                def _():
-                    self.c_own_in().wait_recv()
-
-                self.c_sib(k, p).start()
+            for i in range(CHUNKS):
+                self.ext(i, lambda c: c.start())
+                self.sends(i, lambda c: c.start())
+
+        @pl.when(self.off & self.aside)
+        def _():
+            for i in range(CHUNKS):
+                self.across(i).start()
+
+    def step(self, i):
+        @pl.when(self.on & self.waits)
+        def _():
+            self.near(0, i).wait_recv()
+            self.sends(i, lambda c: c.start())
 
     def arrive(self):
-        @pl.when(self.owner_side)
-        def _():
-            self.c_whole().wait_recv()
-
-        @pl.when(self.side)
-        def _():
-            for k in range(7):
-                dy, dx = OFFSETS[k]
-                self.c_sib(k, peer(self.t, dy, 4 - dx)).wait_recv()
-            self.c_sib(7, self.t).wait_recv()
+        @pl.when(self.off & jnp.logical_not(self.aside))
+        def _():
+            for i in range(CHUNKS):
+                self.sib(i).wait_recv()
 
     def finish(self):
         @pl.when(self.owner)
         def _():
-            for k in range(7):
-                self.c_scatter(k).wait_send()
-                self.c_own(k).wait_send()
-            self.c_whole().wait_send()
-
-        @pl.when(self.relay)
-        def _():
-            for k in range(7):
-                p, c = self.c_ag(k)
-
-                @pl.when(p != self.to)
-                def _():
-                    c.wait_send()
-
-                q, _c = self.c_ag_in(k)
-                self.c_sib(k, q).wait_send()
-            self.c_sib(7, self.t).wait_send()
-
-
-def spread_sems():
+            for i in range(CHUNKS):
+                self.ext(i, lambda c: c.wait_send())
+
+        @pl.when(self.off & self.aside)
+        def _():
+            for i in range(CHUNKS):
+                self.across(i).wait_send()
+
+        @pl.when(self.on)
+        def _():
+            for i in range(CHUNKS):
+                self.sends(i, lambda c: c.wait_send())
+
+
+def tree_sems():
     dma = pltpu.SemaphoreType.DMA
-    return [dma((7,)), dma, dma((7,)), dma, dma((7,)), dma((7,)), dma((8,)), dma((8,))]
+    return [dma((3 * CHUNKS,)), dma((CHUNKS,)), dma((CHUNKS,)), dma((CHUNKS,))]
+
+
+class Ring:
+    PIECES = [
+        ((1, 0), 0), ((0, 3), 0), ((0, 1), 0), ((1, 3), 0), ((1, 1), 0),
+        ((0, 2), 1), ((0, 2), 2), ((1, 2), 1), ((1, 2), 2),
+    ]
+    COPIES = [(-1, 0, 2), (-1, 0, 0), (-1, 0, 1), (0, 0, 0), (0, 0, 1), (1, 1, 0), (2, 2, 1), (3, 1, 0), (4, 2, 1)]
+    NEXT = {0: (3, 4), 1: (5,), 2: (6,), 3: (7,), 4: (8,)}
+
+    def __init__(self, here, buf, rows, start, other, sem):
+        self.here, self.buf, self.rows, self.start_row, self.other_row = here, buf, rows, start, other
+        self.send, self.recv, self.sib_send, self.sib_recv = sem
+
+    def block(self, offset, part, first):
+        q = peer(self.here.t, *offset)
+        row = q * 128 + first
+        rows = self.rows
+        if part:
+            rows = rows // 2
+            row = row + (part - 1) * rows
+        return self.buf.at[pl.ds(pl.multiple_of(row, rows), rows), :]
+
+    def copy(self, n):
+        piece, part, k = self.COPIES[n]
+        offset = (0, 0) if piece < 0 else self.PIECES[piece][0]
+        b = self.block(offset, part, self.start_row)
+        return remote(b, b, self.send.at[n], self.recv.at[n], **self.here.near(k))
+
+    def incoming(self, n):
+        b = self.block(*self.PIECES[n], self.start_row)
+        return remote(b, b, self.send.at[n], self.recv.at[n], **self.here.near(0))
+
+    def sib(self, n, row):
+        b = self.block(*self.PIECES[n], row)
+        return remote(b, b, self.sib_send.at[n], self.sib_recv.at[n], feat=1 - self.here.f)
+
+    def begin(self):
+        for n in (0, 1, 2):
+            self.copy(n).start()
+
+    def step(self, n):
+        self.incoming(n).wait_recv()
+        for m in self.NEXT.get(n, ()):
+            self.copy(m).start()
+        self.sib(n, self.start_row).start()
+
+    def finish(self):
+        for n in range(9):
+            self.copy(n).wait_send()
+            self.sib(n, self.start_row).wait_send()
+
+    def arrive(self):
+        for n in range(9):
+            self.sib(n, self.other_row).wait_recv()
 
 
 def gather_kernel(
     a_ref, y_ref, lab_ref, w_hbm, s_ref, c_ref, yall_ref, labs_ref, inv_ref, w_ref, *sems
 ):
-    s_sem, c_sem, rest = sems[:8], sems[8:16], sems[16:]
-    ysend, yrecv, bsend, brecv, lsend, lrecv, copy_sem = rest
-    t, f, v = lax.axis_index("tm"), lax.axis_index("feat"), lax.axis_index("vox")
+    s_sem, c_sem, y_sem, rest = sems[:4], sems[4:8], sems[8:12], sems[12:]
+    ext_sem, lsend, lrecv, copy_sem, ready = rest
+    here = Place()
+    t, f, v = here.t, here.f, here.v
+    plain, single, server = here.plain, here.single, here.server
     row = t * 2 + f
     to, fo = v // 4, (v // 2) % 2
-    owner_s, owner_c = row == 0, (t == to) & (f == fo)
-    plain, server, single = v != 0, (v == 0) & (f == 1), (v == 0) & (f == 0)
+    owner_s, owner_c = plain & (row == 0), plain & (t == to) & (f == fo)
     barrier = pltpu.get_barrier_semaphore()
 
     def signal(**where):
@@ -169,16 +222,20 @@
 
     @pl.when(plain)
     def _():
-        signal(tm=v // 4, feat=1, vox=0)
+        signal(tm=v // 4, feat=jnp.where(v // 4 == 0, 0, 1), vox=0)
 
     @pl.when(plain | single)
     def _():
-        for dy, dx in OFFSETS:
-            signal(tm=peer(t, dy, dx))
-
-    @pl.when(plain | server)
+        for k in range(3):
+            signal(**here.near(k))
+
+    @pl.when(plain | (server & (t != 0)) | (single & (t == 0)))
     def _():
         signal(feat=1 - f)
+
+    @pl.when(single & (t % 4 == 0))
+    def _():
+        signal(tm=0, feat=0, vox=1)
 
     get_s = pltpu.make_async_copy(a_ref.at[:, pl.ds(0, CB)], s_ref, copy_sem.at[0])
     get_c = pltpu.make_async_copy(
@@ -188,6 +245,7 @@
         y_ref, yall_ref.at[pl.ds(pl.multiple_of(t * 128, 128), 128), :], copy_sem.at[2]
     )
     get_lab = pltpu.make_async_copy(lab_ref, labs_ref, copy_sem.at[3])
+    get_w = pltpu.make_async_copy(w_hbm, w_ref, copy_sem.at[4])
 
     @pl.when(owner_s)
     def _():
@@ -198,12 +256,12 @@
         get_c.start()
 
     get_y.start()
-    get_w = pltpu.make_async_copy(w_hbm, w_ref, copy_sem.at[4])
     get_w.start()
 
     @pl.when(v == 0)
     def _():
         get_lab.start()
+        get_lab.wait()
 
     @pl.when(owner_s)
     def _():
@@ -216,13 +274,19 @@
     get_y.wait()
     get_w.wait()
 
-    @pl.when(v == 0)
-    def _():
-        get_lab.wait()
-
-    @pl.when(plain | single)
-    def _():
-        pl.semaphore_wait(barrier, 8)
+    extra = (v == 1) & (row == 0)
+
+    @pl.when(extra)
+    def _():
+        pl.semaphore_wait(barrier, 6)
+
+    @pl.when((plain & jnp.logical_not(extra)) | (single & (t != 0)))
+    def _():
+        pl.semaphore_wait(barrier, 4)
+
+    @pl.when(single & (t == 0))
+    def _():
+        pl.semaphore_wait(barrier, 3)
 
     @pl.when(server & (t != 0))
     def _():
@@ -230,7 +294,8 @@
 
     @pl.when(server & (t == 0))
     def _():
-        pl.semaphore_wait(barrier, 48)
+        pl.semaphore_wait(barrier, 49)
+        pl.semaphore_signal(ready, inc=1, device_id={"feat": 1}, device_id_type=MESH)
 
     first = jnp.where(t == 0, 16, 0)
 
@@ -244,59 +309,47 @@
         def _(i):
             c_lab(i).start()
 
-    spread_s = Spread(s_ref, t, f, 0, 0, s_sem)
-    spread_c = Spread(c_ref, t, f, to, fo, c_sem)
-    spread_s.start()
-    spread_c.start()
-
-    def yblock(q, g):
-        return yall_ref.at[pl.ds(pl.multiple_of(q * 128 + g * 64, 64), 64), :]
-
-    def yslab(q):
-        return yall_ref.at[pl.ds(pl.multiple_of(q * 128, 128), 128), :]
-
-    def source(k):
-        dy, dx = OFFSETS[k]
-        return peer(t, dy, 4 - dx)
-
-    def c_y(k, b):
-        return remote(b, b, ysend.at[k], yrecv.at[k], tm=peer(t, *OFFSETS[k]))
-
-    def c_yout(k, b):
-        return remote(b, b, bsend.at[k], brecv.at[k], feat=1 - f)
-
-    def y_start(ks):
+    tree_s = Tree(here, s_ref, 0, 0, 0, s_sem, ext_sem)
+    tree_c = Tree(here, c_ref, to, fo, 1, c_sem)
+    halves = Ring(here, yall_ref, 64, f * 64, (1 - f) * 64, y_sem)
+    whole = Ring(here, yall_ref, 128, 0, 0, y_sem)
+
+    def y_do(name, *steps):
         @pl.when(plain)
         def _():
-            for k in ks:
-                c_y(k, yblock(t, f)).start()
+            for n in steps or (None,):
+                getattr(halves, name)(*(() if n is None else (n,)))
 
         @pl.when(single)
         def _():
-            for k in ks:
-                c_y(k, yslab(t)).start()
-
-    def y_collect(ks):
+            for n in steps or (None,):
+                getattr(whole, name)(*(() if n is None else (n,)))
+
+    def c_do(name, *args):
         @pl.when(plain)
         def _():
-            for k in ks:
-                b = yblock(source(k), f)
-                c_y(k, b).wait_recv()
-                c_yout(k, b).start()
-
-        @pl.when(single)
-        def _():
-            for k in ks:
-                b = yslab(source(k))
-                c_y(k, b).wait_recv()
-                c_yout(k, b).start()
-
-    y_start((0, 2))
-    spread_s.forward()
-    spread_c.forward()
-    y_start((3, 1, 4, 6, 5))
-    spread_s.collect()
-    spread_s.arrive()
+            getattr(tree_c, name)(*args)
+
+    tree_s.kick()
+    c_do("kick")
+    y_do("begin")
+
+    @pl.when(single & (t == 0))
+    def _():
+        pl.semaphore_wait(ready, 1)
+
+    tree_s.step(0)
+    c_do("step", 0)
+    tree_s.step(1)
+    c_do("step", 1)
+    y_do("step", 0)
+    tree_s.step(2)
+    c_do("step", 2)
+    y_do("step", 1, 2)
+    tree_s.step(3)
+    c_do("step", 3)
+    y_do("step", 3, 4)
+    tree_s.arrive()
 
     @pl.when(plain)
     def _():
@@ -312,34 +365,28 @@
 
     def between(panel):
         if panel == 0:
-            spread_c.collect()
+            y_do("step", 5, 6)
         elif panel == 1:
-            y_collect((0, 2, 3))
-        elif panel == 2:
-            y_collect((1, 4, 6, 5))
+            y_do("step", 7, 8)
 
     inverse_factor(jnp.stack(matrices), inv_ref, between)
-    spread_c.arrive()
-    spread_s.finish()
-    spread_c.finish()
+    c_do("arrive")
+
+    @pl.when(here.zero)
+    def _():
+        c_ref[...] = s_ref[...]
+
+    tree_s.finish()
+    c_do("finish")
+    y_do("finish")
 
     @pl.when(plain)
     def _():
-        for k in range(7):
-            c_y(k, yblock(t, f)).wait_send()
-            c_yout(k, yblock(source(k), f)).wait_send()
-            c_yout(k, yblock(source(k), 1 - f)).wait_recv()
-
-    @pl.when(single)
-    def _():
-        for k in range(7):
-            c_y(k, yslab(t)).wait_send()
-            c_yout(k, yslab(source(k))).wait_send()
+        halves.arrive()
 
     @pl.when(server)
     def _():
-        for k in range(7):
-            c_yout(k, yslab(source(k))).wait_recv()
+        whole.arrive()
 
         @pl.loop(first, 64)
         def _(i):
@@ -367,9 +414,10 @@
         in_specs=[hbm] * 4,
         out_specs=[vmem] * 5,
         scratch_shapes=[pltpu.SMEM(w.shape, jnp.float32)]
-        + spread_sems()
-        + spread_sems()
-        + [dma((7,)), dma((7,)), dma((7,)), dma((7,)), dma((64,)), dma, dma((5,))],
+        + tree_sems()
+        + tree_sems()
+        + [dma((9,)), dma((9,)), dma((9,)), dma((9,))]
+        + [dma((2 * CHUNKS,)), dma((64,)), dma, dma((5,)), pltpu.SemaphoreType.REGULAR],
         compiler_params=pltpu.CompilerParams(
             collective_id=0, has_side_effects=True, vmem_limit_bytes=24 << 20
         ),

time: 36.1 us -> 37.1 us (1.028)
  the two profiles are of different devices: /device:TPU:1 before, /device:TPU:29 now
where the time goes in v4:
time: 37.1 us; the launch traced here: 36.9 us
  Pallas kernels  36.3 us (98%)
  between operations  0.65 us (2%)
    pallas_call x1, Pallas kernels, gather(): pl.pallas_call(gather_kernel, out_shape=[jax.ShapeDtypeStruct((TIME, CB),...  31.5 us
    pallas_call x1, Pallas kernels, solve(): pl.pallas_call(solve_kernel, out_shape=[jax.ShapeDtypeStruct((2, rows, CB...  4.82 us

profile of v4, /device:TPU:29, one launch (start us, length us, event | category | flops | bytes accessed | tf_op | source)
XLA Modules:
  0.0 36.9 jit_solution(9130361906379550510)
XLA Ops:
  0.6 0.0 copy-start
  0.6 31.5 %gather.1 = (bf16[1024,128]{1,0:T(8,128)(2,1)S(1)}, bf16[1024,128]{1,0:T(8,128)(2,1)S(1)}, bf16[1024,512]{1,0:T(8,128)(2,1)S(1)}, s32[1,128]{1,0:T(1,128)S(1)}, f32[2,128,128]{2,1,0:T(8,128)S(1)}) custom-call(bf16[1024,256]{1,0:T(8,128)(2,1)} %a_ref.3, bf16[128,512]{1,0:T(8,128)(2,1)} %y_ref.1, s32[1,128]{1,0:T(1,128)} %bitcast.1, f32[2,4]{1,0:T(2,128)} %weights_hbm.1), custom_call_target="tpu_custom_call" | custom-call | tf_op jit(solution)/shard_map/gather/pallas_call | solution.py:405
  32.1 0.0 copy-done
  32.1 4.8 %solve.1 = (f32[2,256,128]{2,1,0:T(8,128)}, f32[256,512]{1,0:T(8,128)}) custom-call(f32[2,4]{1,0:T(2,128)} %weights_hbm.1, s32[8]{0:T(128)} %choice_hbm.1, s32[1,128]{1,0:T(1,128)} %bitcast.2, bf16[1024,256]{1,0:T(8,128)(2,1)S(1)} %copy-done, bf16[1024,128]{1,0:T(8,128)(2,1)S(1)} %get-tuple-element.7.s_ref, bf16[1024,128]{1,0:T(8,128)(2,1)S(1)} %get-tuple-element.8.c_ref, ...), custom_call_target="tpu_custom_call" | custom-call | tf_op jit(solution)/shard_map/solve/pallas_call | solution.py:586
Async XLA Ops:
  0.6 31.5 %copy-start = (bf16[1024,256]{1,0:T(8,128)(2,1)S(1)}, bf16[1024,256]{1,0:T(8,128)(2,1)}, u32[]{:S(2)}) copy-start(bf16[1024,256]{1,0:T(8,128)(2,1)} %a_ref.3) | copy-start | bytes 1572868

commit v5 on v3

--- a/solution.py
+++ b/solution.py
@@ -11,7 +11,6 @@
 GROUPS = 4
 CB = 128
 GROUP = 64
-CHIPS = 8
 OFFSETS = [(dy, dx) for dy in range(2) for dx in range(4)][1:]
 MESH = pl.DeviceIdType.MESH
 
@@ -27,14 +26,31 @@
     )
 
 
+class Place:
+    def __init__(self):
+        self.t, self.f, self.v = lax.axis_index("tm"), lax.axis_index("feat"), lax.axis_index("vox")
+        self.zero = self.v == 0
+        self.mover = self.f == jnp.where(self.t == 0, 1, 0)
+        self.plain = self.v != 0
+        self.single = self.zero & self.mover
+        self.server = self.zero & jnp.logical_not(self.mover)
+
+    def core(self, t, own):
+        return jnp.where(self.zero, jnp.where(t == 0, 1, 0), own)
+
+    def chip(self, p):
+        return dict(tm=p, feat=self.core(p, self.f))
+
+
 class Spread:
-    def __init__(self, buf, t, f, to, fo, sem):
-        self.buf, self.t, self.f, self.to, self.fo = buf, t, f, to, fo
+    def __init__(self, here, buf, to, fo, sem):
+        self.here, self.buf, self.t, self.f, self.to = here, buf, here.t, here.f, to
         self.scatter, self.scatter_r, self.own, self.own_r, self.ag, self.ag_r, self.sib, self.sib_r = sem
-        self.owner = (t == to) & (f == fo)
-        self.relay = (t != to) & (f == fo)
-        self.side = (t != to) & (f != fo)
-        self.owner_side = (t == to) & (f != fo)
+        on = self.f == here.core(self.t, fo)
+        self.owner = (self.t == to) & on
+        self.relay = (self.t != to) & on
+        self.side = (self.t != to) & jnp.logical_not(on)
+        self.owner_side = (self.t == to) & jnp.logical_not(on)
 
     def chunk(self, t):
         return self.buf.at[pl.ds(pl.multiple_of(t * 128, 128), 128), :]
@@ -42,31 +58,31 @@
     def c_scatter(self, k):
         p = peer(self.t, *OFFSETS[k])
         c = self.chunk(p)
-        return remote(c, c, self.scatter.at[k], self.scatter_r, tm=p)
+        return remote(c, c, self.scatter.at[k], self.scatter_r, **self.here.chip(p))
 
     def c_scatter_in(self):
         c = self.chunk(self.t)
-        return remote(c, c, self.scatter.at[0], self.scatter_r, tm=self.to)
+        return remote(c, c, self.scatter.at[0], self.scatter_r, **self.here.chip(self.to))
 
     def c_own(self, k):
         p = peer(self.t, *OFFSETS[k])
         c = self.chunk(self.t)
-        return remote(c, c, self.own.at[k], self.own_r, tm=p)
+        return remote(c, c, self.own.at[k], self.own_r, **self.here.chip(p))
 
     def c_own_in(self):
         c = self.chunk(self.to)
-        return remote(c, c, self.own.at[0], self.own_r, tm=self.to)
+        return remote(c, c, self.own.at[0], self.own_r, **self.here.chip(self.to))
 
     def c_ag(self, k):
         p = peer(self.t, *OFFSETS[k])
         c = self.chunk(self.t)
-        return p, remote(c, c, self.ag.at[k], self.ag_r.at[k], tm=p)
+        return p, remote(c, c, self.ag.at[k], self.ag_r.at[k], **self.here.chip(p))
 
     def c_ag_in(self, k):
         dy, dx = OFFSETS[k]
         p = peer(self.t, dy, 4 - dx)
         c = self.chunk(p)
-        return p, remote(c, c, self.ag.at[k], self.ag_r.at[k], tm=p)
+        return p, remote(c, c, self.ag.at[k], self.ag_r.at[k], **self.here.chip(p))
 
     def c_sib(self, k, p):
         c = self.chunk(p)
@@ -82,7 +98,10 @@
                 self.c_scatter(k).start()
             for k in range(7):
                 self.c_own(k).start()
-            self.c_whole().start()
+
+            @pl.when(self.here.plain)
+            def _():
+                self.c_whole().start()
 
     def forward(self):
         @pl.when(self.relay)
@@ -114,7 +133,7 @@
                 self.c_sib(k, p).start()
 
     def arrive(self):
-        @pl.when(self.owner_side)
+        @pl.when(self.owner_side & self.here.plain)
         def _():
             self.c_whole().wait_recv()
 
@@ -131,7 +150,10 @@
             for k in range(7):
                 self.c_scatter(k).wait_send()
                 self.c_own(k).wait_send()
-            self.c_whole().wait_send()
+
+            @pl.when(self.here.plain)
+            def _():
+                self.c_whole().wait_send()
 
         @pl.when(self.relay)
         def _():
@@ -153,15 +175,19 @@
 
 
 def gather_kernel(
-    a_ref, y_ref, lab_ref, w_hbm, s_ref, c_ref, yall_ref, labs_ref, inv_ref, w_ref, *sems
+    a_hbm, y_ref, lab_ref, w_hbm,
+    at_ref, st_ref, grs_ref, grc_ref, gsc_ref, yall_ref, labs_ref, inv_ref,
+    w_ref, a_ref, s_ref, c_ref, *sems,
 ):
     s_sem, c_sem, rest = sems[:8], sems[8:16], sems[16:]
-    ysend, yrecv, bsend, brecv, lsend, lrecv, copy_sem = rest
-    t, f, v = lax.axis_index("tm"), lax.axis_index("feat"), lax.axis_index("vox")
+    ysend, yrecv, bsend, brecv, lsend, lrecv, copy_sem, over_send, over_recv, ready = rest
+    here = Place()
+    t, f, v = here.t, here.f, here.v
+    plain, single, server = here.plain, here.single, here.server
     row = t * 2 + f
     to, fo = v // 4, (v // 2) % 2
-    owner_s, owner_c = row == 0, (t == to) & (f == fo)
-    plain, server, single = v != 0, (v == 0) & (f == 1), (v == 0) & (f == 0)
+    owner_s, owner_c = row == 0, plain & (t == to) & (f == fo)
+    first_single, first_server = single & (t == 0), server & (t == 0)
     barrier = pltpu.get_barrier_semaphore()
 
     def signal(**where):
@@ -169,25 +195,27 @@
 
     @pl.when(plain)
     def _():
-        signal(tm=v // 4, feat=1, vox=0)
+        signal(tm=v // 4, feat=jnp.where(v // 4 == 0, 0, 1), vox=0)
 
     @pl.when(plain | single)
     def _():
-        for dy, dx in OFFSETS:
-            signal(tm=peer(t, dy, dx))
-
-    @pl.when(plain | server)
+        for offset in OFFSETS:
+            signal(**here.chip(peer(t, *offset)))
+
+    @pl.when(plain | (server & (t != 0)) | first_single)
     def _():
         signal(feat=1 - f)
 
-    get_s = pltpu.make_async_copy(a_ref.at[:, pl.ds(0, CB)], s_ref, copy_sem.at[0])
+    get_s = pltpu.make_async_copy(a_hbm.at[:, pl.ds(0, CB)], s_ref, copy_sem.at[0])
     get_c = pltpu.make_async_copy(
-        a_ref.at[:, pl.ds(pl.multiple_of((v % 2) * CB, CB), CB)], c_ref, copy_sem.at[1]
+        a_hbm.at[:, pl.ds(pl.multiple_of((v % 2) * CB, CB), CB)], c_ref, copy_sem.at[1]
     )
     get_y = pltpu.make_async_copy(
         y_ref, yall_ref.at[pl.ds(pl.multiple_of(t * 128, 128), 128), :], copy_sem.at[2]
     )
     get_lab = pltpu.make_async_copy(lab_ref, labs_ref, copy_sem.at[3])
+    get_w = pltpu.make_async_copy(w_hbm, w_ref, copy_sem.at[4])
+    get_a = pltpu.make_async_copy(a_hbm, a_ref, copy_sem.at[5])
 
     @pl.when(owner_s)
     def _():
@@ -198,12 +226,13 @@
         get_c.start()
 
     get_y.start()
-    get_w = pltpu.make_async_copy(w_hbm, w_ref, copy_sem.at[4])
     get_w.start()
+    get_a.start()
 
     @pl.when(v == 0)
     def _():
         get_lab.start()
+        get_lab.wait()
 
     @pl.when(owner_s)
     def _():
@@ -215,22 +244,28 @@
 
     get_y.wait()
     get_w.wait()
-
-    @pl.when(v == 0)
-    def _():
-        get_lab.wait()
-
-    @pl.when(plain | single)
+    get_a.wait()
+    at_ref[...] = a_ref[...].T
+
+    @pl.when(plain | (single & (t != 0)))
     def _():
         pl.semaphore_wait(barrier, 8)
 
+    @pl.when(first_single)
+    def _():
+        pl.semaphore_wait(barrier, 7)
+
     @pl.when(server & (t != 0))
     def _():
         pl.semaphore_wait(barrier, 64)
 
-    @pl.when(server & (t == 0))
-    def _():
-        pl.semaphore_wait(barrier, 48)
+    over = remote(s_ref, s_ref, over_send, over_recv, feat=1 - f)
+
+    @pl.when(first_server)
+    def _():
+        pl.semaphore_wait(barrier, 49)
+        pl.semaphore_signal(ready, inc=1, device_id={"feat": 1}, device_id_type=MESH)
+        over.start()
 
     first = jnp.where(t == 0, 16, 0)
 
@@ -244,10 +279,19 @@
         def _(i):
             c_lab(i).start()
 
-    spread_s = Spread(s_ref, t, f, 0, 0, s_sem)
-    spread_c = Spread(c_ref, t, f, to, fo, c_sem)
-    spread_s.start()
-    spread_c.start()
+    spread_s = Spread(here, s_ref, 0, 0, s_sem)
+    spread_c = Spread(here, c_ref, to, fo, c_sem)
+
+    def c_do(name):
+        @pl.when(plain)
+        def _():
+            getattr(spread_c, name)()
+
+    @pl.when(plain)
+    def _():
+        spread_s.start()
+
+    c_do("start")
 
     def yblock(q, g):
         return yall_ref.at[pl.ds(pl.multiple_of(q * 128 + g * 64, 64), 64), :]
@@ -260,7 +304,7 @@
         return peer(t, dy, 4 - dx)
 
     def c_y(k, b):
-        return remote(b, b, ysend.at[k], yrecv.at[k], tm=peer(t, *OFFSETS[k]))
+        return remote(b, b, ysend.at[k], yrecv.at[k], **here.chip(peer(t, *OFFSETS[k])))
 
     def c_yout(k, b):
         return remote(b, b, bsend.at[k], brecv.at[k], feat=1 - f)
@@ -292,9 +336,21 @@
                 c_yout(k, b).start()
 
     y_start((0, 2))
+
+    @pl.when(first_single)
+    def _():
+        y_start((3, 1, 4, 6, 5))
+        pl.semaphore_wait(ready, 1)
+        over.wait_recv()
+        spread_s.start()
+
     spread_s.forward()
-    spread_c.forward()
-    y_start((3, 1, 4, 6, 5))
+    c_do("forward")
+
+    @pl.when(jnp.logical_not(first_single))
+    def _():
+        y_start((3, 1, 4, 6, 5))
+
     spread_s.collect()
     spread_s.arrive()
 
@@ -303,7 +359,8 @@
         c_lab(0).wait_recv()
 
     s_all = s_ref[...]
-    gram = tdot(s_all, s_all) * (1.0 / TIME)
+    st_ref[...] = s_all.T
+    gram = dot(st_ref[...], s_all) * (1.0 / TIME)
     eye = lax.broadcasted_iota(jnp.int32, (CB, CB), 0) == lax.broadcasted_iota(jnp.int32, (CB, CB), 1)
     matrices = []
     for r in range(2):
@@ -312,16 +369,29 @@
 
     def between(panel):
         if panel == 0:
-            spread_c.collect()
+            c_do("collect")
         elif panel == 1:
             y_collect((0, 2, 3))
         elif panel == 2:
             y_collect((1, 4, 6, 5))
 
     inverse_factor(jnp.stack(matrices), inv_ref, between)
-    spread_c.arrive()
+    grs_ref[...] = dot(at_ref[...], s_all) * (1.0 / TIME)
+    c_do("arrive")
+
+    @pl.when(here.zero)
+    def _():
+        c_ref[...] = s_ref[...]
+
+    c_all = c_ref[...]
+    grc_ref[...] = dot(at_ref[...], c_all) * (1.0 / TIME)
+    gsc_ref[...] = dot(st_ref[...], c_all) * (1.0 / TIME)
     spread_s.finish()
-    spread_c.finish()
+    c_do("finish")
+
+    @pl.when(first_server)
+    def _():
+        over.wait_send()
 
     @pl.when(plain)
     def _():
@@ -354,22 +424,31 @@
     dma = pltpu.SemaphoreType.DMA
     vmem = pl.BlockSpec(memory_space=pltpu.VMEM)
     hbm = pl.BlockSpec(memory_space=pltpu.HBM)
-    voxels = y.shape[1]
+    rows, voxels = a.shape[1], y.shape[1]
     return pl.pallas_call(
         gather_kernel,
         out_shape=[
-            jax.ShapeDtypeStruct((TIME, CB), jnp.bfloat16),
-            jax.ShapeDtypeStruct((TIME, CB), jnp.bfloat16),
+            jax.ShapeDtypeStruct((rows, TIME), jnp.bfloat16),
+            jax.ShapeDtypeStruct((CB, TIME), jnp.bfloat16),
+            jax.ShapeDtypeStruct((rows, CB), jnp.float32),
+            jax.ShapeDtypeStruct((rows, CB), jnp.float32),
+            jax.ShapeDtypeStruct((CB, CB), jnp.float32),
             jax.ShapeDtypeStruct((TIME, voxels), jnp.bfloat16),
             jax.ShapeDtypeStruct((1, CB), jnp.int32),
             jax.ShapeDtypeStruct((2, CB, CB), jnp.float32),
         ],
         in_specs=[hbm] * 4,
-        out_specs=[vmem] * 5,
-        scratch_shapes=[pltpu.SMEM(w.shape, jnp.float32)]
+        out_specs=[vmem] * 8,
+        scratch_shapes=[
+            pltpu.SMEM(w.shape, jnp.float32),
+            pltpu.VMEM(a.shape, jnp.bfloat16),
+            pltpu.VMEM((TIME, CB), jnp.bfloat16),
+            pltpu.VMEM((TIME, CB), jnp.bfloat16),
+        ]
         + spread_sems()
         + spread_sems()
-        + [dma((7,)), dma((7,)), dma((7,)), dma((7,)), dma((64,)), dma, dma((5,))],
+        + [dma((7,)), dma((7,)), dma((7,)), dma((7,)), dma((64,)), dma, dma((6,))]
+        + [dma, dma, pltpu.SemaphoreType.REGULAR],
         compiler_params=pltpu.CompilerParams(
             collective_id=0, has_side_effects=True, vmem_limit_bytes=24 << 20
         ),
@@ -466,13 +545,27 @@
     return lax.dot_general(a, b, (((0,), (0,)), ((), ())), preferred_element_type=jnp.float32)
 
 
-def fdot(a, b):
-    return jnp.dot(a, b, precision=lax.Precision.HIGHEST, preferred_element_type=jnp.float32)
+def stack_left(x):
+    h, m, l = parts(x)
+    return jnp.concatenate([h, h, h, m, m, l], axis=1)
+
+
+def stack_right(x, axis):
+    h, m, l = parts(x)
+    return jnp.concatenate([h, m, l, h, m, h], axis=axis)
+
+
+def dot(a, b):
+    return jnp.dot(a, b, preferred_element_type=jnp.float32)
+
+
+def dot_nt(a, b):
+    return lax.dot_general(a, b, (((1,), (1,)), ((), ())), preferred_element_type=jnp.float32)
 
 
 def solve_kernel(
-    weights_hbm, choice_hbm, labc_hbm, a_ref, s_ref, c_ref, y_ref, labs_ref, inv_ref, trail_ref, sides_ref,
-    weights_ref, choice_ref, labc_ref, sem
+    weights_hbm, choice_hbm, labc_hbm, at_ref, st_ref, grs_ref, grc_ref, gsc_ref, y_ref, labs_ref, inv_ref,
+    trail_ref, sides_ref, weights_ref, choice_ref, labc_ref, sem,
 ):
     small = [
         pltpu.make_async_copy(weights_hbm, weights_ref, sem.at[0]),
@@ -484,24 +577,15 @@
     t, f, v = lax.axis_index("tm"), lax.axis_index("feat"), lax.axis_index("vox")
     row = t * 2 + f
     rows, voxels = sides_ref.shape
-    s = s_ref[...]
-    c = c_ref[...]
     y = y_ref[...]
-    a = a_ref[...]
-
-    i_sub = lax.broadcasted_iota(jnp.int32, (CB, CB), 0)
-    i_lane = lax.broadcasted_iota(jnp.int32, (CB, CB), 1)
-    eye = i_sub == i_lane
+    sside = dot(st_ref[...], y) * (1.0 / math.sqrt(TIME))
+    sside6 = stack_right(sside, 0)
     for copy in small:
         copy.wait()
+
+    eye = lax.broadcasted_iota(jnp.int32, (CB, CB), 0) == lax.broadcasted_iota(jnp.int32, (CB, CB), 1)
     r_sub = lax.broadcasted_iota(jnp.int32, (rows, CB), 0) + row * rows
     r_lane = lax.broadcasted_iota(jnp.int32, (rows, CB), 1)
-    grs = tdot(a, s) * (1.0 / TIME)
-    grc = tdot(a, c) * (1.0 / TIME)
-    gsc = tdot(s, c) * (1.0 / TIME)
-    side = tdot(a, y) * (1.0 / math.sqrt(TIME))
-    sside = tdot(s, y) * (1.0 / math.sqrt(TIME))
-
     group = lax.broadcasted_iota(jnp.int32, (1, voxels), 1) // GROUP
     ridge = jnp.zeros((1, voxels), jnp.int32)
     for g in range(voxels // GROUP):
@@ -510,38 +594,38 @@
     panels, solved = [], []
     for r in range(2):
         inv = inv_ref[r]
+        left = stack_left(inv)
         pen_s = jnp.broadcast_to(penalty(weights_ref, r, labs_ref[...]), (rows, CB))
         pen_c = jnp.broadcast_to(penalty(weights_ref, r, labc_ref[...]), (rows, CB))
-        grs_r = grs + jnp.where(r_sub == r_lane, pen_s, 0.0)
-        gsc_r = gsc + jnp.where(eye & (v == 0), pen_c[:CB], 0.0)
-        panel = lax.dot_general(
-            grs_r, inv, (((1,), (1,)), ((), ())), precision=lax.Precision.HIGHEST,
-            preferred_element_type=jnp.float32,
-        )
-        partner = fdot(inv, gsc_r)
-        system = grc + jnp.where(r_sub == r_lane + v * CB, pen_c, 0.0)
-        trail_ref[r] = system - fdot(panel, partner)
+        grs_r = grs_ref[...] + jnp.where(r_sub == r_lane, pen_s, 0.0)
+        gsc_r = gsc_ref[...] + jnp.where(eye & (v == 0), pen_c[:CB], 0.0)
+        panel = stack_left(dot_nt(stack_left(grs_r), stack_right(inv, 1)))
+        partner = dot(left, stack_right(gsc_r, 0))
+        system = grc_ref[...] + jnp.where(r_sub == r_lane + v * CB, pen_c, 0.0)
+        trail_ref[r] = system - dot(panel, stack_right(partner, 0))
         panels.append(panel)
-        solved.append(jnp.where(ridge == r, fdot(inv, sside), 0.0))
-    update = fdot(panels[0], solved[0]) + fdot(panels[1], solved[1])
-    sides_ref[...] = side - update
+        solved.append(jnp.where(ridge == r, dot(left, sside6), 0.0))
+    update = dot(
+        jnp.concatenate(panels, 1), jnp.concatenate([stack_right(solved[0], 0), stack_right(solved[1], 0)], 0)
+    )
+    sides_ref[...] = dot(at_ref[...], y) * (1.0 / math.sqrt(TIME)) - update
 
     @pl.when(row == 0)
     def _():
         sides_ref[0:CB, :] = solved[0] + solved[1]
 
 
-def solve(weights, choice, labc, a, s, c, y, labs, inv):
+def solve(weights, choice, labc, at, st, grs, grc, gsc, y, labs, inv):
     vmem = pl.BlockSpec(memory_space=pltpu.VMEM)
     hbm = pl.BlockSpec(memory_space=pltpu.HBM)
-    rows, voxels = a.shape[1], y.shape[1]
+    rows, voxels = at.shape[0], y.shape[1]
     return pl.pallas_call(
         solve_kernel,
         out_shape=[
             jax.ShapeDtypeStruct((2, rows, CB), jnp.float32),
             jax.ShapeDtypeStruct((rows, voxels), jnp.float32),
         ],
-        in_specs=[hbm] * 3 + [vmem] * 6,
+        in_specs=[hbm] * 3 + [vmem] * 8,
         out_specs=[vmem] * 2,
         scratch_shapes=[
             pltpu.SMEM(weights.shape, jnp.float32),
@@ -551,14 +635,13 @@
         ],
         compiler_params=pltpu.CompilerParams(vmem_limit_bytes=32 << 20),
         name="solve",
-    )(*in_hbm(weights, choice, labc), a, s, c, y, labs, inv)
+    )(*in_hbm(weights, choice, labc), at, st, grs, grc, gsc, y, labs, inv)
 
 
 def local(design, signals, label, weights, choice):
     lab = label.reshape(1, CB)
-    s, c, y, labs, inv = gather(design, signals, lab, weights)
-    trail, sides = solve(weights, choice, lab, design, s, c, y, labs, inv)
-    return trail, sides
+    at, st, grs, grc, gsc, y, labs, inv = gather(design, signals, lab, weights)
+    return solve(weights, choice, lab, at, st, grs, grc, gsc, y, labs, inv)
 
 
 def solution(mesh):

time: 36.1 us -> 37.8 us (1.047)
  the two profiles are of different devices: /device:TPU:1 before, /device:TPU:5 now
where the time goes in v5:
time: 37.8 us; the launch traced here: 37.6 us
  Pallas kernels  37 us (98%)
  between operations  0.64 us (2%)
    pallas_call x1, Pallas kernels, gather(): pl.pallas_call(gather_kernel, out_shape=[jax.ShapeDtypeStruct((rows, TIME...  33.3 us
    pallas_call x1, Pallas kernels, solve(): pl.pallas_call(solve_kernel, out_shape=[jax.ShapeDtypeStruct((2, rows, CB...  3.64 us

profile of v5, /device:TPU:5, one launch (start us, length us, event | category | flops | bytes accessed | tf_op | source)
XLA Modules:
  0.0 37.6 jit_solution(3246196989031665684)
XLA Ops:
  0.6 33.3 %gather.1 = (bf16[256,1024]{1,0:T(8,128)(2,1)S(1)}, bf16[128,1024]{1,0:T(8,128)(2,1)S(1)}, f32[256,128]{1,0:T(8,128)S(1)}, f32[256,128]{1,0:T(8,128)S(1)}, f32[1...) custom-call(bf16[1024,256]{1,0:T(8,128)(2,1)} %a_hbm.1, ...), custom_call_target="tpu_custom_call" | custom-call | tf_op jit(solution)/shard_map/gather/pallas_call | solution.py:428
  34.0 3.6 %solve.1 = (f32[2,256,128]{2,1,0:T(8,128)}, f32[256,512]{1,0:T(8,128)}) custom-call(f32[2,4]{1,0:T(2,128)} %weights_hbm.1, s32[8]{0:T(128)} %choice_hbm.1, s32[1,128]{1,0:T(1,128)} %bitcast.2, bf16[256,1024]{1,0:T(8,128)(2,1)S(1)} %get-tuple-element.10.at_ref, bf16[128,1024]{1,0:T(8,128)(2,1)S(1)} %get-tuple-element.11.st_ref, ...), custom_call_target="tpu_custom_call" | custom-call | tf_op jit(solution)/shard_map/solve/pallas_call | solution.py:622

commit v6 on v5

--- a/solution.py
+++ b/solution.py
@@ -43,8 +43,10 @@
 
 
 class Spread:
-    def __init__(self, here, buf, to, fo, sem):
-        self.here, self.buf, self.t, self.f, self.to = here, buf, here.t, here.f, to
+    def __init__(self, here, buf, to, fo, sem, extra=None):
+        self.here, self.buf, self.t, self.f, self.extra = here, buf, here.t, here.f, extra
+        to = jnp.where(here.zero, -1, to)
+        self.to = to
         self.scatter, self.scatter_r, self.own, self.own_r, self.ag, self.ag_r, self.sib, self.sib_r = sem
         on = self.f == here.core(self.t, fo)
         self.owner = (self.t == to) & on
@@ -91,6 +93,15 @@
     def c_whole(self):
         return remote(self.buf, self.buf, self.sib.at[0], self.sib_r.at[0], feat=1 - self.f)
 
+    def pass_on(self, act):
+        if self.extra is not None:
+
+            @pl.when(self.here.v == 1)
+            def _():
+                c = self.chunk(self.t)
+                feat = jnp.where(self.t == 0, 1, 0)
+                act(remote(c, c, self.extra, self.scatter_r, feat=feat, vox=0))
+
     def start(self):
         @pl.when(self.owner)
         def _():
@@ -98,15 +109,14 @@
                 self.c_scatter(k).start()
             for k in range(7):
                 self.c_own(k).start()
-
-            @pl.when(self.here.plain)
-            def _():
-                self.c_whole().start()
+            self.c_whole().start()
+            self.pass_on(lambda c: c.start())
 
     def forward(self):
         @pl.when(self.relay)
         def _():
             self.c_scatter_in().wait_recv()
+            self.pass_on(lambda c: c.start())
             for k in range(7):
                 p, c = self.c_ag(k)
 
@@ -133,7 +143,7 @@
                 self.c_sib(k, p).start()
 
     def arrive(self):
-        @pl.when(self.owner_side & self.here.plain)
+        @pl.when(self.owner_side)
         def _():
             self.c_whole().wait_recv()
 
@@ -150,10 +160,8 @@
             for k in range(7):
                 self.c_scatter(k).wait_send()
                 self.c_own(k).wait_send()
-
-            @pl.when(self.here.plain)
-            def _():
-                self.c_whole().wait_send()
+            self.c_whole().wait_send()
+            self.pass_on(lambda c: c.wait_send())
 
         @pl.when(self.relay)
         def _():
@@ -167,6 +175,7 @@
                 q, _c = self.c_ag_in(k)
                 self.c_sib(k, q).wait_send()
             self.c_sib(7, self.t).wait_send()
+            self.pass_on(lambda c: c.wait_send())
 
 
 def spread_sems():
@@ -180,13 +189,13 @@
     w_ref, a_ref, s_ref, c_ref, *sems,
 ):
     s_sem, c_sem, rest = sems[:8], sems[8:16], sems[16:]
-    ysend, yrecv, bsend, brecv, lsend, lrecv, copy_sem, over_send, over_recv, ready = rest
+    ysend, yrecv, bsend, brecv, lsend, lrecv, copy_sem, extra_sem, ready = rest
     here = Place()
     t, f, v = here.t, here.f, here.v
     plain, single, server = here.plain, here.single, here.server
     row = t * 2 + f
     to, fo = v // 4, (v // 2) % 2
-    owner_s, owner_c = row == 0, plain & (t == to) & (f == fo)
+    owner_s, owner_c = plain & (row == 0), plain & (t == to) & (f == fo)
     first_single, first_server = single & (t == 0), server & (t == 0)
     barrier = pltpu.get_barrier_semaphore()
 
@@ -205,6 +214,12 @@
     @pl.when(plain | (server & (t != 0)) | first_single)
     def _():
         signal(feat=1 - f)
+
+    extra = (v == 1) & (f == 0)
+
+    @pl.when(single)
+    def _():
+        signal(feat=0, vox=1)
 
     get_s = pltpu.make_async_copy(a_hbm.at[:, pl.ds(0, CB)], s_ref, copy_sem.at[0])
     get_c = pltpu.make_async_copy(
@@ -244,10 +259,20 @@
 
     get_y.wait()
     get_w.wait()
-    get_a.wait()
-    at_ref[...] = a_ref[...].T
-
-    @pl.when(plain | (single & (t != 0)))
+
+    def transpose():
+        get_a.wait()
+        at_ref[...] = a_ref[...].T
+
+    @pl.when(plain | single)
+    def _():
+        transpose()
+
+    @pl.when(extra)
+    def _():
+        pl.semaphore_wait(barrier, 9)
+
+    @pl.when((plain & jnp.logical_not(extra)) | (single & (t != 0)))
     def _():
         pl.semaphore_wait(barrier, 8)
 
@@ -258,14 +283,11 @@
     @pl.when(server & (t != 0))
     def _():
         pl.semaphore_wait(barrier, 64)
-
-    over = remote(s_ref, s_ref, over_send, over_recv, feat=1 - f)
 
     @pl.when(first_server)
     def _():
         pl.semaphore_wait(barrier, 49)
         pl.semaphore_signal(ready, inc=1, device_id={"feat": 1}, device_id_type=MESH)
-        over.start()
 
     first = jnp.where(t == 0, 16, 0)
 
@@ -279,7 +301,9 @@
         def _(i):
             c_lab(i).start()
 
-    spread_s = Spread(here, s_ref, 0, 0, s_sem)
+        transpose()
+
+    spread_s = Spread(here, s_ref, 0, 0, s_sem, extra_sem)
     spread_c = Spread(here, c_ref, to, fo, c_sem)
 
     def c_do(name):
@@ -287,10 +311,7 @@
         def _():
             getattr(spread_c, name)()
 
-    @pl.when(plain)
-    def _():
-        spread_s.start()
-
+    spread_s.start()
     c_do("start")
 
     def yblock(q, g):
@@ -339,17 +360,11 @@
 
     @pl.when(first_single)
     def _():
-        y_start((3, 1, 4, 6, 5))
         pl.semaphore_wait(ready, 1)
-        over.wait_recv()
-        spread_s.start()
 
     spread_s.forward()
     c_do("forward")
-
-    @pl.when(jnp.logical_not(first_single))
-    def _():
-        y_start((3, 1, 4, 6, 5))
+    y_start((3, 1, 4, 6, 5))
 
     spread_s.collect()
     spread_s.arrive()
@@ -388,10 +403,6 @@
     gsc_ref[...] = dot(st_ref[...], c_all) * (1.0 / TIME)
     spread_s.finish()
     c_do("finish")
-
-    @pl.when(first_server)
-    def _():
-        over.wait_send()
 
     @pl.when(plain)
     def _():
@@ -448,7 +459,7 @@
         + spread_sems()
         + spread_sems()
         + [dma((7,)), dma((7,)), dma((7,)), dma((7,)), dma((64,)), dma, dma((6,))]
-        + [dma, dma, pltpu.SemaphoreType.REGULAR],
+        + [dma, pltpu.SemaphoreType.REGULAR],
         compiler_params=pltpu.CompilerParams(
             collective_id=0, has_side_effects=True, vmem_limit_bytes=24 << 20
         ),

time: 37.8 us -> 38.2 us (1.011)
  Pallas kernels: 37 us -> 37.4 us
    pallas_call x1, Pallas kernels: 33.3 us -> 33.8 us  [gather(): pl.pallas_call(gather_kernel, out_shape=[jax.ShapeDtypeStruct((rows, TIME...]
where the time goes in v6:
time: 38.2 us; the launch traced here: 38.1 us
  Pallas kernels  37.4 us (98%)
  between operations  0.64 us (2%)
    pallas_call x1, Pallas kernels, gather(): pl.pallas_call(gather_kernel, out_shape=[jax.ShapeDtypeStruct((rows, TIME...  33.8 us
    pallas_call x1, Pallas kernels, solve(): pl.pallas_call(solve_kernel, out_shape=[jax.ShapeDtypeStruct((2, rows, CB...  3.64 us

profile of v6, /device:TPU:5, one launch (start us, length us, event | category | flops | bytes accessed | tf_op | source)
XLA Modules:
  0.0 38.1 jit_solution(6609015380629965584)
XLA Ops:
  0.6 33.8 %gather.1 = (bf16[256,1024]{1,0:T(8,128)(2,1)S(1)}, bf16[128,1024]{1,0:T(8,128)(2,1)S(1)}, f32[256,128]{1,0:T(8,128)S(1)}, f32[256,128]{1,0:T(8,128)S(1)}, f32[1...) custom-call(bf16[1024,256]{1,0:T(8,128)(2,1)} %a_hbm.1, ...), custom_call_target="tpu_custom_call" | custom-call | tf_op jit(solution)/shard_map/gather/pallas_call | solution.py:439
  34.4 3.6 %solve.1 = (f32[2,256,128]{2,1,0:T(8,128)}, f32[256,512]{1,0:T(8,128)}) custom-call(f32[2,4]{1,0:T(2,128)} %weights_hbm.1, s32[8]{0:T(128)} %choice_hbm.1, s32[1,128]{1,0:T(1,128)} %bitcast.2, bf16[256,1024]{1,0:T(8,128)(2,1)S(1)} %get-tuple-element.10.at_ref, bf16[128,1024]{1,0:T(8,128)(2,1)S(1)} %get-tuple-element.11.st_ref, ...), custom_call_target="tpu_custom_call" | custom-call | tf_op jit(solution)/shard_map/solve/pallas_call | solution.py:633

commit v7 on v6

--- a/solution.py
+++ b/solution.py
@@ -26,29 +26,11 @@
     )
 
 
-class Place:
-    def __init__(self):
-        self.t, self.f, self.v = lax.axis_index("tm"), lax.axis_index("feat"), lax.axis_index("vox")
-        self.zero = self.v == 0
-        self.mover = self.f == jnp.where(self.t == 0, 1, 0)
-        self.plain = self.v != 0
-        self.single = self.zero & self.mover
-        self.server = self.zero & jnp.logical_not(self.mover)
-
-    def core(self, t, own):
-        return jnp.where(self.zero, jnp.where(t == 0, 1, 0), own)
-
-    def chip(self, p):
-        return dict(tm=p, feat=self.core(p, self.f))
-
-
 class Spread:
-    def __init__(self, here, buf, to, fo, sem, extra=None):
-        self.here, self.buf, self.t, self.f, self.extra = here, buf, here.t, here.f, extra
-        to = jnp.where(here.zero, -1, to)
-        self.to = to
+    def __init__(self, buf, t, f, to, fo, sem):
+        self.buf, self.t, self.f, self.to = buf, t, f, to
         self.scatter, self.scatter_r, self.own, self.own_r, self.ag, self.ag_r, self.sib, self.sib_r = sem
-        on = self.f == here.core(self.t, fo)
+        on = f == fo
         self.owner = (self.t == to) & on
         self.relay = (self.t != to) & on
         self.side = (self.t != to) & jnp.logical_not(on)
@@ -60,31 +42,31 @@
     def c_scatter(self, k):
         p = peer(self.t, *OFFSETS[k])
         c = self.chunk(p)
-        return remote(c, c, self.scatter.at[k], self.scatter_r, **self.here.chip(p))
+        return remote(c, c, self.scatter.at[k], self.scatter_r, tm=p)
 
     def c_scatter_in(self):
         c = self.chunk(self.t)
-        return remote(c, c, self.scatter.at[0], self.scatter_r, **self.here.chip(self.to))
+        return remote(c, c, self.scatter.at[0], self.scatter_r, tm=self.to)
 
     def c_own(self, k):
         p = peer(self.t, *OFFSETS[k])
         c = self.chunk(self.t)
-        return remote(c, c, self.own.at[k], self.own_r, **self.here.chip(p))
+        return remote(c, c, self.own.at[k], self.own_r, tm=p)
 
     def c_own_in(self):
         c = self.chunk(self.to)
-        return remote(c, c, self.own.at[0], self.own_r, **self.here.chip(self.to))
+        return remote(c, c, self.own.at[0], self.own_r, tm=self.to)
 
     def c_ag(self, k):
         p = peer(self.t, *OFFSETS[k])
         c = self.chunk(self.t)
-        return p, remote(c, c, self.ag.at[k], self.ag_r.at[k], **self.here.chip(p))
+        return p, remote(c, c, self.ag.at[k], self.ag_r.at[k], tm=p)
 
     def c_ag_in(self, k):
         dy, dx = OFFSETS[k]
         p = peer(self.t, dy, 4 - dx)
         c = self.chunk(p)
-        return p, remote(c, c, self.ag.at[k], self.ag_r.at[k], **self.here.chip(p))
+        return p, remote(c, c, self.ag.at[k], self.ag_r.at[k], tm=p)
 
     def c_sib(self, k, p):
         c = self.chunk(p)
@@ -93,15 +75,6 @@
     def c_whole(self):
         return remote(self.buf, self.buf, self.sib.at[0], self.sib_r.at[0], feat=1 - self.f)
 
-    def pass_on(self, act):
-        if self.extra is not None:
-
-            @pl.when(self.here.v == 1)
-            def _():
-                c = self.chunk(self.t)
-                feat = jnp.where(self.t == 0, 1, 0)
-                act(remote(c, c, self.extra, self.scatter_r, feat=feat, vox=0))
-
     def start(self):
         @pl.when(self.owner)
         def _():
@@ -110,13 +83,11 @@
             for k in range(7):
                 self.c_own(k).start()
             self.c_whole().start()
-            self.pass_on(lambda c: c.start())
 
     def forward(self):
         @pl.when(self.relay)
         def _():
             self.c_scatter_in().wait_recv()
-            self.pass_on(lambda c: c.start())
             for k in range(7):
                 p, c = self.c_ag(k)
 
@@ -161,7 +132,6 @@
                 self.c_scatter(k).wait_send()
                 self.c_own(k).wait_send()
             self.c_whole().wait_send()
-            self.pass_on(lambda c: c.wait_send())
 
         @pl.when(self.relay)
         def _():
@@ -175,7 +145,6 @@
                 q, _c = self.c_ag_in(k)
                 self.c_sib(k, q).wait_send()
             self.c_sib(7, self.t).wait_send()
-            self.pass_on(lambda c: c.wait_send())
 
 
 def spread_sems():
@@ -189,37 +158,33 @@
     w_ref, a_ref, s_ref, c_ref, *sems,
 ):
     s_sem, c_sem, rest = sems[:8], sems[8:16], sems[16:]
-    ysend, yrecv, bsend, brecv, lsend, lrecv, copy_sem, extra_sem, ready = rest
-    here = Place()
-    t, f, v = here.t, here.f, here.v
-    plain, single, server = here.plain, here.single, here.server
+    ysend, yrecv, bsend, brecv, lsend, lrecv, copy_sem, ready = rest
+    t, f, v = lax.axis_index("tm"), lax.axis_index("feat"), lax.axis_index("vox")
     row = t * 2 + f
     to, fo = v // 4, (v // 2) % 2
-    owner_s, owner_c = plain & (row == 0), plain & (t == to) & (f == fo)
-    first_single, first_server = single & (t == 0), server & (t == 0)
+    other = v != 0
+    server = (v == 0) & (f == 1)
+    owner_s, owner_c = row == 0, other & (t == to) & (f == fo)
+    last_in = (v == 0) & (row == 0)
     barrier = pltpu.get_barrier_semaphore()
 
     def signal(**where):
         pl.semaphore_signal(barrier, inc=1, device_id=where, device_id_type=MESH)
 
-    @pl.when(plain)
-    def _():
-        signal(tm=v // 4, feat=jnp.where(v // 4 == 0, 0, 1), vox=0)
-
-    @pl.when(plain | single)
-    def _():
-        for offset in OFFSETS:
-            signal(**here.chip(peer(t, *offset)))
-
-    @pl.when(plain | (server & (t != 0)) | first_single)
-    def _():
-        signal(feat=1 - f)
-
-    extra = (v == 1) & (f == 0)
-
-    @pl.when(single)
-    def _():
-        signal(feat=0, vox=1)
+    for offset in OFFSETS:
+        signal(tm=peer(t, *offset))
+    signal(feat=1 - f)
+
+    first = jnp.where(t == 0, 16, 0)
+
+    def client(i):
+        return dict(tm=i // 2 % 8, feat=i % 2, vox=t * 4 + i // 16)
+
+    @pl.when(server)
+    def _():
+        @pl.loop(first, 64)
+        def _(i):
+            signal(**client(i))
 
     get_s = pltpu.make_async_copy(a_hbm.at[:, pl.ds(0, CB)], s_ref, copy_sem.at[0])
     get_c = pltpu.make_async_copy(
@@ -264,36 +229,78 @@
         get_a.wait()
         at_ref[...] = a_ref[...].T
 
-    @pl.when(plain | single)
+    @pl.when(jnp.logical_not(last_in))
     def _():
         transpose()
 
-    @pl.when(extra)
+    @pl.when(v == 0)
+    def _():
+        pl.semaphore_wait(barrier, 8)
+
+    @pl.when(other)
     def _():
         pl.semaphore_wait(barrier, 9)
-
-    @pl.when((plain & jnp.logical_not(extra)) | (single & (t != 0)))
-    def _():
-        pl.semaphore_wait(barrier, 8)
-
-    @pl.when(first_single)
-    def _():
-        pl.semaphore_wait(barrier, 7)
+        pl.semaphore_signal(
+            ready, inc=1, device_id={"tm": v // 4, "feat": 1, "vox": 0}, device_id_type=MESH
+        )
+
+    def c_lab(i):
+        return remote(labs_ref, labs_ref, lsend.at[i], lrecv, **client(i))
+
+    spread_s = Spread(s_ref, t, f, 0, 0, s_sem)
+    spread_c = Spread(c_ref, t, f, to, fo, c_sem)
+
+    def c_do(name):
+        @pl.when(other)
+        def _():
+            getattr(spread_c, name)()
+
+    spread_s.start()
+    c_do("start")
+
+    def yblock(q, g):
+        return yall_ref.at[pl.ds(pl.multiple_of(q * 128 + g * 64, 64), 64), :]
+
+    def source(k):
+        dy, dx = OFFSETS[k]
+        return peer(t, dy, 4 - dx)
+
+    def c_y(k, b):
+        return remote(b, b, ysend.at[k], yrecv.at[k], tm=peer(t, *OFFSETS[k]))
+
+    def c_yout(k, b):
+        return remote(b, b, bsend.at[k], brecv.at[k], feat=1 - f)
+
+    def y_start(ks):
+        for k in ks:
+            c_y(k, yblock(t, f)).start()
+
+    def y_collect(ks):
+        for k in ks:
+            b = yblock(source(k), f)
+            c_y(k, b).wait_recv()
+            c_yout(k, b).start()
+
+    y_start((0, 2))
+
+    @pl.when(last_in)
+    def _():
+        transpose()
+
+    spread_s.forward()
+    c_do("forward")
+    y_start((3, 1, 4, 6, 5))
+
+    spread_s.collect()
+    spread_s.arrive()
 
     @pl.when(server & (t != 0))
     def _():
-        pl.semaphore_wait(barrier, 64)
-
-    @pl.when(first_server)
-    def _():
-        pl.semaphore_wait(barrier, 49)
-        pl.semaphore_signal(ready, inc=1, device_id={"feat": 1}, device_id_type=MESH)
-
-    first = jnp.where(t == 0, 16, 0)
-
-    def c_lab(i):
-        where = dict(tm=i // 2 % 8, feat=i % 2, vox=t * 4 + i // 16)
-        return remote(labs_ref, labs_ref, lsend.at[i], lrecv, **where)
+        pl.semaphore_wait(ready, 64)
+
+    @pl.when(server & (t == 0))
+    def _():
+        pl.semaphore_wait(ready, 48)
 
     @pl.when(server)
     def _():
@@ -301,75 +308,7 @@
         def _(i):
             c_lab(i).start()
 
-        transpose()
-
-    spread_s = Spread(here, s_ref, 0, 0, s_sem, extra_sem)
-    spread_c = Spread(here, c_ref, to, fo, c_sem)
-
-    def c_do(name):
-        @pl.when(plain)
-        def _():
-            getattr(spread_c, name)()
-
-    spread_s.start()
-    c_do("start")
-
-    def yblock(q, g):
-        return yall_ref.at[pl.ds(pl.multiple_of(q * 128 + g * 64, 64), 64), :]
-
-    def yslab(q):
-        return yall_ref.at[pl.ds(pl.multiple_of(q * 128, 128), 128), :]
-
-    def source(k):
-        dy, dx = OFFSETS[k]
-        return peer(t, dy, 4 - dx)
-
-    def c_y(k, b):
-        return remote(b, b, ysend.at[k], yrecv.at[k], **here.chip(peer(t, *OFFSETS[k])))
-
-    def c_yout(k, b):
-        return remote(b, b, bsend.at[k], brecv.at[k], feat=1 - f)
-
-    def y_start(ks):
-        @pl.when(plain)
-        def _():
-            for k in ks:
-                c_y(k, yblock(t, f)).start()
-
-        @pl.when(single)
-        def _():
-            for k in ks:
-                c_y(k, yslab(t)).start()
-
-    def y_collect(ks):
-        @pl.when(plain)
-        def _():
-            for k in ks:
-                b = yblock(source(k), f)
-                c_y(k, b).wait_recv()
-                c_yout(k, b).start()
-
-        @pl.when(single)
-        def _():
-            for k in ks:
-                b = yslab(source(k))
-                c_y(k, b).wait_recv()
-                c_yout(k, b).start()
-
-    y_start((0, 2))
-
-    @pl.when(first_single)
-    def _():
-        pl.semaphore_wait(ready, 1)
-
-    spread_s.forward()
-    c_do("forward")
-    y_start((3, 1, 4, 6, 5))
-
-    spread_s.collect()
-    spread_s.arrive()
-
-    @pl.when(plain)
+    @pl.when(other)
     def _():
         c_lab(0).wait_recv()
 
@@ -394,7 +333,7 @@
     grs_ref[...] = dot(at_ref[...], s_all) * (1.0 / TIME)
     c_do("arrive")
 
-    @pl.when(here.zero)
+    @pl.when(v == 0)
     def _():
         c_ref[...] = s_ref[...]
 
@@ -404,24 +343,13 @@
     spread_s.finish()
     c_do("finish")
 
-    @pl.when(plain)
-    def _():
-        for k in range(7):
-            c_y(k, yblock(t, f)).wait_send()
-            c_yout(k, yblock(source(k), f)).wait_send()
-            c_yout(k, yblock(source(k), 1 - f)).wait_recv()
-
-    @pl.when(single)
-    def _():
-        for k in range(7):
-            c_y(k, yslab(t)).wait_send()
-            c_yout(k, yslab(source(k))).wait_send()
+    for k in range(7):
+        c_y(k, yblock(t, f)).wait_send()
+        c_yout(k, yblock(source(k), f)).wait_send()
+        c_yout(k, yblock(source(k), 1 - f)).wait_recv()
 
     @pl.when(server)
     def _():
-        for k in range(7):
-            c_yout(k, yslab(source(k))).wait_recv()
-
         @pl.loop(first, 64)
         def _(i):
             c_lab(i).wait_send()
@@ -459,7 +387,7 @@
         + spread_sems()
         + spread_sems()
         + [dma((7,)), dma((7,)), dma((7,)), dma((7,)), dma((64,)), dma, dma((6,))]
-        + [dma, pltpu.SemaphoreType.REGULAR],
+        + [pltpu.SemaphoreType.REGULAR],
         compiler_params=pltpu.CompilerParams(
             collective_id=0, has_side_effects=True, vmem_limit_bytes=24 << 20
         ),

time: 38.2 us -> 34.1 us (0.89)
  the two profiles are of different devices: /device:TPU:5 before, /device:TPU:17 now
where the time goes in v7:
time: 34.1 us; the launch traced here: 33.9 us
  Pallas kernels  33.3 us (98%)
  between operations  0.64 us (2%)
    pallas_call x1, Pallas kernels, gather(): pl.pallas_call(gather_kernel, out_shape=[jax.ShapeDtypeStruct((rows, TIME...  29.6 us
    pallas_call x1, Pallas kernels, solve(): pl.pallas_call(solve_kernel, out_shape=[jax.ShapeDtypeStruct((2, rows, CB...  3.64 us

profile of v7, /device:TPU:17, one launch (start us, length us, event | category | flops | bytes accessed | tf_op | source)
XLA Modules:
  0.0 33.9 jit_solution(4822037109673942227)
XLA Ops:
  0.6 29.6 %gather.1 = (bf16[256,1024]{1,0:T(8,128)(2,1)S(1)}, bf16[128,1024]{1,0:T(8,128)(2,1)S(1)}, f32[256,128]{1,0:T(8,128)S(1)}, f32[256,128]{1,0:T(8,128)S(1)}, f32[1...) custom-call(bf16[1024,256]{1,0:T(8,128)(2,1)} %a_hbm.1, ...), custom_call_target="tpu_custom_call" | custom-call | tf_op jit(solution)/shard_map/gather/pallas_call | solution.py:367
  30.3 3.6 %solve.1 = (f32[2,256,128]{2,1,0:T(8,128)}, f32[256,512]{1,0:T(8,128)}) custom-call(f32[2,4]{1,0:T(2,128)} %weights_hbm.1, s32[8]{0:T(128)} %choice_hbm.1, s32[1,128]{1,0:T(1,128)} %bitcast.2, bf16[256,1024]{1,0:T(8,128)(2,1)S(1)} %get-tuple-element.10.at_ref, bf16[128,1024]{1,0:T(8,128)(2,1)S(1)} %get-tuple-element.11.st_ref, ...), custom_call_target="tpu_custom_call" | custom-call | tf_op jit(solution)/shard_map/solve/pallas_call | solution.py:561

commit v8 on v7

--- a/solution.py
+++ b/solution.py
@@ -27,8 +27,8 @@
 
 
 class Spread:
-    def __init__(self, buf, t, f, to, fo, sem):
-        self.buf, self.t, self.f, self.to = buf, t, f, to
+    def __init__(self, buf, t, f, to, fo, sem, v=None, extra=None):
+        self.buf, self.t, self.f, self.to, self.v, self.extra = buf, t, f, to, v, extra
         self.scatter, self.scatter_r, self.own, self.own_r, self.ag, self.ag_r, self.sib, self.sib_r = sem
         on = f == fo
         self.owner = (self.t == to) & on
@@ -75,11 +75,29 @@
     def c_whole(self):
         return remote(self.buf, self.buf, self.sib.at[0], self.sib_r.at[0], feat=1 - self.f)
 
+    def scatter_all(self, act):
+        if self.v is None:
+            for k in range(7):
+                act(self.c_scatter(k))
+        else:
+
+            @pl.when(self.v != 0)
+            def _():
+                for k in range(7):
+                    act(self.c_scatter(k))
+
+    def pass_on(self, act):
+        if self.v is not None:
+
+            @pl.when(self.v == 1)
+            def _():
+                c = self.chunk(self.t)
+                act(remote(c, c, self.extra, self.scatter_r, vox=0))
+
     def start(self):
         @pl.when(self.owner)
         def _():
-            for k in range(7):
-                self.c_scatter(k).start()
+            self.scatter_all(lambda c: c.start())
             for k in range(7):
                 self.c_own(k).start()
             self.c_whole().start()
@@ -88,6 +106,7 @@
         @pl.when(self.relay)
         def _():
             self.c_scatter_in().wait_recv()
+            self.pass_on(lambda c: c.start())
             for k in range(7):
                 p, c = self.c_ag(k)
 
@@ -128,8 +147,8 @@
     def finish(self):
         @pl.when(self.owner)
         def _():
+            self.scatter_all(lambda c: c.wait_send())
             for k in range(7):
-                self.c_scatter(k).wait_send()
                 self.c_own(k).wait_send()
             self.c_whole().wait_send()
 
@@ -145,6 +164,7 @@
                 q, _c = self.c_ag_in(k)
                 self.c_sib(k, q).wait_send()
             self.c_sib(7, self.t).wait_send()
+            self.pass_on(lambda c: c.wait_send())
 
 
 def spread_sems():
@@ -158,7 +178,7 @@
     w_ref, a_ref, s_ref, c_ref, *sems,
 ):
     s_sem, c_sem, rest = sems[:8], sems[8:16], sems[16:]
-    ysend, yrecv, bsend, brecv, lsend, lrecv, copy_sem, ready = rest
+    ysend, yrecv, bsend, brecv, lsend, lrecv, copy_sem, extra_sem, ready = rest
     t, f, v = lax.axis_index("tm"), lax.axis_index("feat"), lax.axis_index("vox")
     row = t * 2 + f
     to, fo = v // 4, (v // 2) % 2
@@ -174,6 +194,13 @@
     for offset in OFFSETS:
         signal(tm=peer(t, *offset))
     signal(feat=1 - f)
+
+    helped = (v == 0) & (f == 0) & (t != 0)
+    helper = (v == 1) & (f == 0) & (t != 0)
+
+    @pl.when(helped)
+    def _():
+        signal(vox=1)
 
     first = jnp.where(t == 0, 16, 0)
 
@@ -237,9 +264,16 @@
     def _():
         pl.semaphore_wait(barrier, 8)
 
+    @pl.when(helper)
+    def _():
+        pl.semaphore_wait(barrier, 10)
+
+    @pl.when(other & jnp.logical_not(helper))
+    def _():
+        pl.semaphore_wait(barrier, 9)
+
     @pl.when(other)
     def _():
-        pl.semaphore_wait(barrier, 9)
         pl.semaphore_signal(
             ready, inc=1, device_id={"tm": v // 4, "feat": 1, "vox": 0}, device_id_type=MESH
         )
@@ -247,7 +281,7 @@
     def c_lab(i):
         return remote(labs_ref, labs_ref, lsend.at[i], lrecv, **client(i))
 
-    spread_s = Spread(s_ref, t, f, 0, 0, s_sem)
+    spread_s = Spread(s_ref, t, f, 0, 0, s_sem, v, extra_sem)
     spread_c = Spread(c_ref, t, f, to, fo, c_sem)
 
     def c_do(name):
@@ -387,7 +421,7 @@
         + spread_sems()
         + spread_sems()
         + [dma((7,)), dma((7,)), dma((7,)), dma((7,)), dma((64,)), dma, dma((6,))]
-        + [pltpu.SemaphoreType.REGULAR],
+        + [dma, pltpu.SemaphoreType.REGULAR],
         compiler_params=pltpu.CompilerParams(
             collective_id=0, has_side_effects=True, vmem_limit_bytes=24 << 20
         ),

time: 34.1 us -> 37.6 us (1.10)
  the two profiles are of different devices: /device:TPU:17 before, /device:TPU:169 now
where the time goes in v8:
time: 37.6 us; the launch traced here: 37.4 us
  Pallas kernels  36.8 us (98%)
  between operations  0.64 us (2%)
    pallas_call x1, Pallas kernels, gather(): pl.pallas_call(gather_kernel, out_shape=[jax.ShapeDtypeStruct((rows, TIME...  33.2 us
    pallas_call x1, Pallas kernels, solve(): pl.pallas_call(solve_kernel, out_shape=[jax.ShapeDtypeStruct((2, rows, CB...  3.64 us

profile of v8, /device:TPU:169, one launch (start us, length us, event | category | flops | bytes accessed | tf_op | source)
XLA Modules:
  0.0 37.4 jit_solution(13780402432283827241)
XLA Ops:
  0.6 33.2 %gather.1 = (bf16[256,1024]{1,0:T(8,128)(2,1)S(1)}, bf16[128,1024]{1,0:T(8,128)(2,1)S(1)}, f32[256,128]{1,0:T(8,128)S(1)}, f32[256,128]{1,0:T(8,128)S(1)}, f32[1...) custom-call(bf16[1024,256]{1,0:T(8,128)(2,1)} %a_hbm.1, ...), custom_call_target="tpu_custom_call" | custom-call | tf_op jit(solution)/shard_map/gather/pallas_call | solution.py:401
  33.8 3.6 %solve.1 = (f32[2,256,128]{2,1,0:T(8,128)}, f32[256,512]{1,0:T(8,128)}) custom-call(f32[2,4]{1,0:T(2,128)} %weights_hbm.1, s32[8]{0:T(128)} %choice_hbm.1, s32[1,128]{1,0:T(1,128)} %bitcast.2, bf16[256,1024]{1,0:T(8,128)(2,1)S(1)} %get-tuple-element.10.at_ref, bf16[128,1024]{1,0:T(8,128)(2,1)S(1)} %get-tuple-element.11.st_ref, ...), custom_call_target="tpu_custom_call" | custom-call | tf_op jit(solution)/shard_map/solve/pallas_call | solution.py:595

commit v9 on v7

--- a/solution.py
+++ b/solution.py
@@ -281,18 +281,13 @@
             c_y(k, b).wait_recv()
             c_yout(k, b).start()
 
-    y_start((0, 2))
-
     @pl.when(last_in)
     def _():
         transpose()
 
     spread_s.forward()
     c_do("forward")
-    y_start((3, 1, 4, 6, 5))
-
-    spread_s.collect()
-    spread_s.arrive()
+    y_start((0, 2, 3, 1, 4, 6, 5))
 
     @pl.when(server & (t != 0))
     def _():
@@ -307,6 +302,10 @@
         @pl.loop(first, 64)
         def _(i):
             c_lab(i).start()
+
+
+    spread_s.collect()
+    spread_s.arrive()
 
     @pl.when(other)
     def _():

time: 34.1 us -> 34.1 us (level)
  no operation moved by 1% of the time
where the time goes in v9:
time: 34.1 us; the launch traced here: 33.9 us
  Pallas kernels  33.3 us (98%)
  between operations  0.64 us (2%)
    pallas_call x1, Pallas kernels, gather(): pl.pallas_call(gather_kernel, out_shape=[jax.ShapeDtypeStruct((rows, TIME...  29.6 us
    pallas_call x1, Pallas kernels, solve(): pl.pallas_call(solve_kernel, out_shape=[jax.ShapeDtypeStruct((2, rows, CB...  3.64 us

profile of v9, /device:TPU:17, one launch (start us, length us, event | category | flops | bytes accessed | tf_op | source)
XLA Modules:
  0.0 33.9 jit_solution(8601442549318374286)
XLA Ops:
  0.6 29.6 %gather.1 = (bf16[256,1024]{1,0:T(8,128)(2,1)S(1)}, bf16[128,1024]{1,0:T(8,128)(2,1)S(1)}, f32[256,128]{1,0:T(8,128)S(1)}, f32[256,128]{1,0:T(8,128)S(1)}, f32[1...) custom-call(bf16[1024,256]{1,0:T(8,128)(2,1)} %a_hbm.1, ...), custom_call_target="tpu_custom_call" | custom-call | tf_op jit(solution)/shard_map/gather/pallas_call | solution.py:366
  30.3 3.6 %solve.1 = (f32[2,256,128]{2,1,0:T(8,128)}, f32[256,512]{1,0:T(8,128)}) custom-call(f32[2,4]{1,0:T(2,128)} %weights_hbm.1, s32[8]{0:T(128)} %choice_hbm.1, s32[1,128]{1,0:T(1,128)} %bitcast.2, bf16[256,1024]{1,0:T(8,128)(2,1)S(1)} %get-tuple-element.10.at_ref, bf16[128,1024]{1,0:T(8,128)(2,1)S(1)} %get-tuple-element.11.st_ref, ...), custom_call_target="tpu_custom_call" | custom-call | tf_op jit(solution)/shard_map/solve/pallas_call | solution.py:560

commit v10 on v9

--- a/solution.py
+++ b/solution.py
@@ -329,16 +329,21 @@
             y_collect((1, 4, 6, 5))
 
     inverse_factor(jnp.stack(matrices), inv_ref, between)
-    grs_ref[...] = dot(at_ref[...], s_all) * (1.0 / TIME)
+    grs = dot(at_ref[...], s_all) * (1.0 / TIME)
+    grs_ref[...] = grs
     c_do("arrive")
 
     @pl.when(v == 0)
     def _():
-        c_ref[...] = s_ref[...]
-
-    c_all = c_ref[...]
-    grc_ref[...] = dot(at_ref[...], c_all) * (1.0 / TIME)
-    gsc_ref[...] = dot(st_ref[...], c_all) * (1.0 / TIME)
+        grc_ref[...] = grs
+        gsc_ref[...] = gram
+
+    @pl.when(other)
+    def _():
+        c_all = c_ref[...]
+        grc_ref[...] = dot(at_ref[...], c_all) * (1.0 / TIME)
+        gsc_ref[...] = dot(st_ref[...], c_all) * (1.0 / TIME)
+
     spread_s.finish()
     c_do("finish")
 

time: 34.1 us -> 33.7 us (0.988)
  Pallas kernels: 33.3 us -> 32.9 us
    pallas_call x1, Pallas kernels: 29.6 us -> 29.3 us  [gather(): pl.pallas_call(gather_kernel, out_shape=[jax.ShapeDtypeStruct((rows, TIME...]
where the time goes in v10:
time: 33.7 us; the launch traced here: 33.6 us
  Pallas kernels  32.9 us (98%)
  between operations  0.64 us (2%)
    pallas_call x1, Pallas kernels, gather(): pl.pallas_call(gather_kernel, out_shape=[jax.ShapeDtypeStruct((rows, TIME...  29.3 us
    pallas_call x1, Pallas kernels, solve(): pl.pallas_call(solve_kernel, out_shape=[jax.ShapeDtypeStruct((2, rows, CB...  3.64 us

profile of v10, /device:TPU:17, one launch (start us, length us, event | category | flops | bytes accessed | tf_op | source)
XLA Modules:
  0.0 33.6 jit_solution(6755402286780632771)
XLA Ops:
  0.6 29.3 %gather.1 = (bf16[256,1024]{1,0:T(8,128)(2,1)S(1)}, bf16[128,1024]{1,0:T(8,128)(2,1)S(1)}, f32[256,128]{1,0:T(8,128)S(1)}, f32[256,128]{1,0:T(8,128)S(1)}, f32[1...) custom-call(bf16[1024,256]{1,0:T(8,128)(2,1)} %a_hbm.1, ...), custom_call_target="tpu_custom_call" | custom-call | tf_op jit(solution)/shard_map/gather/pallas_call | solution.py:371
  29.9 3.6 %solve.1 = (f32[2,256,128]{2,1,0:T(8,128)}, f32[256,512]{1,0:T(8,128)}) custom-call(f32[2,4]{1,0:T(2,128)} %weights_hbm.1, s32[8]{0:T(128)} %choice_hbm.1, s32[1,128]{1,0:T(1,128)} %bitcast.2, bf16[256,1024]{1,0:T(8,128)(2,1)S(1)} %get-tuple-element.10.at_ref, bf16[128,1024]{1,0:T(8,128)(2,1)S(1)} %get-tuple-element.11.st_ref, ...), custom_call_target="tpu_custom_call" | custom-call | tf_op jit(solution)/shard_map/solve/pallas_call | solution.py:565

commit v11 on v10

--- a/solution.py
+++ b/solution.py
@@ -75,11 +75,20 @@
     def c_whole(self):
         return remote(self.buf, self.buf, self.sib.at[0], self.sib_r.at[0], feat=1 - self.f)
 
-    def start(self):
-        @pl.when(self.owner)
+    def scatter_from(self, source):
+        for k in range(7):
+            p = peer(self.t, *OFFSETS[k])
+            rows = source.at[pl.ds(pl.multiple_of(p * 128, 128), 128), pl.ds(0, CB)]
+            remote(rows, self.chunk(p), self.scatter.at[k], self.scatter_r, tm=p).start()
+
+    def start(self, scattered):
+        @pl.when(self.owner & jnp.logical_not(scattered))
         def _():
             for k in range(7):
                 self.c_scatter(k).start()
+
+        @pl.when(self.owner)
+        def _():
             for k in range(7):
                 self.c_own(k).start()
             self.c_whole().start()
@@ -205,6 +214,14 @@
     def _():
         get_c.start()
 
+    spread_s = Spread(s_ref, t, f, 0, 0, s_sem)
+    spread_c = Spread(c_ref, t, f, to, fo, c_sem)
+
+    @pl.when(last_in)
+    def _():
+        pl.semaphore_wait(barrier, 8)
+        spread_s.scatter_from(a_hbm)
+
     get_y.start()
     get_w.start()
     get_a.start()
@@ -233,7 +250,7 @@
     def _():
         transpose()
 
-    @pl.when(v == 0)
+    @pl.when((v == 0) & jnp.logical_not(last_in))
     def _():
         pl.semaphore_wait(barrier, 8)
 
@@ -247,16 +264,14 @@
     def c_lab(i):
         return remote(labs_ref, labs_ref, lsend.at[i], lrecv, **client(i))
 
-    spread_s = Spread(s_ref, t, f, 0, 0, s_sem)
-    spread_c = Spread(c_ref, t, f, to, fo, c_sem)
-
-    def c_do(name):
+
+    def c_do(name, *args):
         @pl.when(other)
         def _():
-            getattr(spread_c, name)()
-
-    spread_s.start()
-    c_do("start")
+            getattr(spread_c, name)(*args)
+
+    spread_s.start(last_in)
+    c_do("start", False)
 
     def yblock(q, g):
         return yall_ref.at[pl.ds(pl.multiple_of(q * 128 + g * 64, 64), 64), :]

time: 33.7 us -> 33.7 us (level)
  no operation moved by 1% of the time
where the time goes in v11:
time: 33.7 us; the launch traced here: 33.6 us
  Pallas kernels  32.9 us (98%)
  between operations  0.64 us (2%)
    pallas_call x1, Pallas kernels, gather(): pl.pallas_call(gather_kernel, out_shape=[jax.ShapeDtypeStruct((rows, TIME...  29.3 us
    pallas_call x1, Pallas kernels, solve(): pl.pallas_call(solve_kernel, out_shape=[jax.ShapeDtypeStruct((2, rows, CB...  3.64 us

profile of v11, /device:TPU:17, one launch (start us, length us, event | category | flops | bytes accessed | tf_op | source)
XLA Modules:
  0.0 33.6 jit_solution(18114664987604978673)
XLA Ops:
  0.6 29.3 %gather.1 = (bf16[256,1024]{1,0:T(8,128)(2,1)S(1)}, bf16[128,1024]{1,0:T(8,128)(2,1)S(1)}, f32[256,128]{1,0:T(8,128)S(1)}, f32[256,128]{1,0:T(8,128)S(1)}, f32[1...) custom-call(bf16[1024,256]{1,0:T(8,128)(2,1)} %a_hbm.1, ...), custom_call_target="tpu_custom_call" | custom-call | tf_op jit(solution)/shard_map/gather/pallas_call | solution.py:386
  29.9 3.6 %solve.1 = (f32[2,256,128]{2,1,0:T(8,128)}, f32[256,512]{1,0:T(8,128)}) custom-call(f32[2,4]{1,0:T(2,128)} %weights_hbm.1, s32[8]{0:T(128)} %choice_hbm.1, s32[1,128]{1,0:T(1,128)} %bitcast.2, bf16[256,1024]{1,0:T(8,128)(2,1)S(1)} %get-tuple-element.10.at_ref, bf16[128,1024]{1,0:T(8,128)(2,1)S(1)} %get-tuple-element.11.st_ref, ...), custom_call_target="tpu_custom_call" | custom-call | tf_op jit(solution)/shard_map/solve/pallas_call | solution.py:580
